TPU v7x, 512 devices: a whole 4x8x8 slice. The times are simulated.
512 devices in a mesh: member: 8 (over z_hi, core), grid: 64 (over x, z_lo, y).
Axes of the slice: x: 4, y: 8, z: 8 (z_hi: 4, z_lo: 2; z = z_hi * 2 + z_lo), core: 2. Of those that a mesh axis runs over, the one named last changes fastest.
Arguments:
- mesh_latent: bfloat16 [8, 512, 8192], P('member', None, 'grid'), may hold values from -6 to 6
- grid_latent: bfloat16 [8, 512, 65536], P('member', None, 'grid'), may hold values from -6 to 6
- edge_sources: int32 [3, 65536], P(None, 'grid'), may hold values from 0 to 8191, as said below
- edge_weights: bfloat16 [3, 65536], P(None, 'grid'), may hold values from 0.19921875 to 1
- area_weight: float32 [65536], P('grid'), may hold values from 0.3 to 1.7
- band_counts: int32 [64], P('grid'), may hold values from 256 to 1024, as said below
- target: bfloat16 [100, 65536], P(None, 'grid'), may hold values from -3 to 3
- hidden_weight: bfloat16 [512, 512], replicated, may hold values from -0.25 to 0.25
- out_weight: bfloat16 [512, 100], replicated, may hold values from -0.25 to 0.25
Outputs:
- grad_hidden_weight: float32 [512, 512], P('grid')
- grad_out_weight: float32 [512, 100], P('grid')
- grad_mesh: float32 [8, 512, 8192], P('member', None, 'grid')
Inputs may be any that keep to these rules, and one draw needn't show every extreme that they name: `edge_sources`: the 3 nodes of one grid point are distinct and lie in its own band's nodes or within 64 nodes on either side of them; band b holds nodes b * 128 to (b + 1) * 128 - 1 and grid slots b * 1024 to (b + 1) * 1024 - 1. `band_counts`: some band is full.
All inputs are finite; a program needn't handle non-finite values.
Results may differ from a plain program's by a relative error of at most 0.04.
Values may be sent and summed in bfloat16 or wider, within the bound.
A program may use at most 64 MiB of HBM per device.

v0:
```python
import jax
import jax.numpy as jnp
from jax import lax
from jax.sharding import PartitionSpec as P

HALO = 64
EDGES = 3


smooth_sq = 0.01
loss_scale = 4096.0


def with_halo(value, sides, width):
    for axis, dim in sides:
        devices, length = (lax.axis_size(axis), value.shape[dim])
        up = [(i, (i + 1) % devices) for i in range(devices - 1)]
        down = [(j, i) for i, j in up]
        last = lax.slice_in_dim(value, length - width, length, axis=dim)
        first = lax.slice_in_dim(value, 0, width, axis=dim)
        before = lax.ppermute(last, axis, up)
        after = lax.ppermute(first, axis, down)
        value = jnp.concatenate([before, value, after], axis=dim)
    return value


def from_behind(value, axis, steps):
    count = lax.axis_size(axis)
    first, last = (max(0, -steps), min(count, count - steps))
    return lax.ppermute(value, axis, [(source, source + steps) for source in range(first, last)])


def slope(diff):
    return diff / jnp.sqrt(diff * diff + smooth_sq)


def local(
    mesh_latent,
    grid_latent,
    edge_sources,
    edge_weights,
    area_weight,
    band_counts,
    target,
    hidden_weight,
    out_weight,
):
    members = lax.axis_size("member")
    node_count = mesh_latent.shape[2]
    points = grid_latent.shape[2]
    width = hidden_weight.shape[0]
    band = lax.axis_index("grid")
    extended = with_halo(mesh_latent, (("grid", 2),), HALO)[0]
    local_src = edge_sources - (band * node_count - HALO)
    slots = jnp.arange(node_count + 2 * HALO, dtype=jnp.int32)
    adjacency = jnp.zeros((node_count + 2 * HALO, points), jnp.float32)
    for k in range(EDGES):
        adjacency = adjacency + jnp.where(
            local_src[k][None, :] == slots[:, None],
            edge_weights[k].astype(jnp.float32)[None, :],
            0.0,
        )
    adjacency = adjacency.astype(jnp.bfloat16)
    agg = jnp.dot(extended, adjacency, preferred_element_type=jnp.float32)
    x_in = (agg + grid_latent[0].astype(jnp.float32)).astype(jnp.bfloat16)
    pre = lax.dot_general(
        hidden_weight, x_in, (((0,), (0,)), ((), ())), preferred_element_type=jnp.float32
    )
    sig = jax.nn.sigmoid(pre)
    hidden = (pre * sig).astype(jnp.bfloat16)
    pred = lax.dot_general(
        out_weight, hidden, (((0,), (0,)), ((), ())), preferred_element_type=jnp.float32
    ).astype(jnp.bfloat16)
    pred_f = pred.astype(jnp.float32)
    own = slope(pred_f - target.astype(jnp.float32))
    pair = jnp.sum(
        slope(
            pred_f[None]
            - lax.all_gather(pred[None], "member", axis=0, tiled=True).astype(jnp.float32)
        ),
        axis=0,
    )
    live = (jnp.arange(points, dtype=jnp.int32) < band_counts[0]).astype(jnp.float32)
    coef = loss_scale * area_weight * live / target.shape[0]
    gpred = (coef[None, :] * (own / members - pair / (members * (members - 1)))).astype(
        jnp.bfloat16
    )
    dh = jnp.dot(out_weight, gpred, preferred_element_type=jnp.float32)
    dpre = (dh * sig * (1.0 + pre * (1.0 - sig))).astype(jnp.bfloat16)
    dx = jnp.dot(hidden_weight, dpre, preferred_element_type=jnp.float32).astype(jnp.bfloat16)
    ext_grad = lax.dot_general(
        dx, adjacency, (((1,), (1,)), ((), ())), preferred_element_type=jnp.float32
    )
    from_above = from_behind(ext_grad[:, :HALO], "grid", -1)
    from_below = from_behind(ext_grad[:, node_count + HALO :], "grid", 1)
    node_grad = ext_grad[:, HALO : HALO + node_count]
    node_grad = node_grad.at[:, node_count - HALO :].add(from_above)
    node_grad = node_grad.at[:, :HALO].add(from_below)
    first = lax.dot_general(
        x_in, dpre, (((1,), (1,)), ((), ())), preferred_element_type=jnp.float32
    )
    second = lax.dot_general(
        hidden, gpred, (((1,), (1,)), ((), ())), preferred_element_type=jnp.float32
    )
    shard = lax.psum_scatter(
        jnp.concatenate([first, second], axis=1), "grid", scatter_dimension=0, tiled=True
    )
    summed = lax.psum(shard, "member")
    return (summed[:, :width], summed[:, width:], node_grad[None])


def solution(mesh):
    return jax.shard_map(
        local,
        mesh=mesh,
        in_specs=(
            P("member", None, "grid"),
            P("member", None, "grid"),
            P(None, "grid"),
            P(None, "grid"),
            P("grid"),
            P("grid"),
            P(None, "grid"),
            P(),
            P(),
        ),
        out_specs=(P("grid", None), P("grid", None), P("member", None, "grid")),
        check_vma=False,
    )
```

profile of v0, /device:TPU:1, one launch (start us, length us, event | category | flops | bytes accessed | tf_op | source)
XLA Modules:
  0.0 700.3 jit_solution(15300585780270853451)
XLA Ops:
  7.2 0.0 copy-start
  7.2 0.0 all-gather.4.cloned.1.call-start
  7.2 1.1 fusion.25
  8.3 4.0 collective-permute-start
  12.4 1.3 collective-permute-start.1
  13.7 0.7 broadcast_subtract_fusion
  14.4 0.8 slice_convert_fusion.2
  15.3 0.0 collective-permute-done
  15.3 2.8 collective-permute-done.1
  18.1 2.1 fusion.5
  20.2 0.0 copy-done
  20.2 0.0 copy-start.5
  20.2 0.0 copy-start.3
  20.2 0.0 copy-start.4
  20.2 2.3 fusion.11
  22.5 0.0 copy-done.5
  22.5 0.0 copy-done.3
  22.5 0.0 copy-start.2
  22.5 1.1 bitcast_convert_fusion
  23.7 0.0 copy-start.1
  23.7 0.0 all-gather.4.cloned.1.call-update
  23.7 0.0 all-reduce.3.cloned.1.call-start
  24.4 0.0 copy-done.4
  24.5 43.4 %all-gather.4.cloned.1.call-done = bf16[8,100,1024]{2,1,0:T(8,128)(2,1)} async-done(((bf16[1,100,1024]{2,1,0:T(8,128)(2,1)}), bf16[8,100,1024]{2,1,0:T(8,128)(2,1)}) %all-gather.4.cloned.1.call-update) | async-done | bytes 1638416 | tf_op jit(solution)/shard_map/all_gather | solution.py:79
  67.9 0.0 copy-start.7
  67.9 2.4 fusion.4
  70.3 0.0 copy-done.2
  70.3 0.0 copy-done.1
  70.4 0.2 multiply_convert_fusion
  70.5 0.3 fusion.28
  70.8 0.0 copy-done.7
  70.8 0.0 copy-start.6
  70.8 0.9 fusion.7
  71.8 0.3 copy-done.6
  72.1 0.8 fusion.27
  72.8 1.1 pad_maximum_fusion
  74.0 0.0 all-reduce.3.cloned.1.call-update
  74.0 1.1 fusion.13
  75.2 1.3 collective-permute-start.2
  76.5 1.3 dynamic-slice.16
  78.4 0.6 compare_reduce_fusion
  79.0 4.0 collective-permute-start.3
  83.0 0.0 collective-permute-done.2
  83.1 2.3 collective-permute-done.3
  85.4 0.7 fusion.19
  86.0 0.8 copy.17
  86.9 535.5 %all-reduce.3.cloned.1.call-done = f32[512,612]{0,1:T(8,128)} async-done(((f32[512,612]{0,1:T(8,128)}), f32[512,612]{0,1:T(8,128)}) %all-reduce.3.cloned.1.call-update) | async-done | bytes 1253392
  622.4 1.1 constant_dynamic-slice_fusion
  623.5 68.5 %psum.7 = f32[8,612]{0,1:T(8,128)S(1)} all-reduce(f32[8,612]{0,1:T(8,128)S(1)} %constant_dynamic-slice_fusion), channel_id=1, replica_groups=mesh['member'=8,'grid'=64] {'member'}, use_global_device_ids=true, to_apply=%region_2.3 | all-reduce | flops 4896 | bytes 39168 | tf_op jit(solution)/shard_map/psum | solution.py:108
  692.1 0.7 copy.15
  692.8 0.7 copy.16
  (8 shorter events, 0.1 us)
Async XLA Ops:
  7.2 13.0 %copy-start = (bf16[512,512]{1,0:T(8,128)(2,1)S(1)}, bf16[512,512]{1,0:T(8,128)(2,1)}, u32[]{:S(2)}) copy-start(bf16[512,512]{1,0:T(8,128)(2,1)} %param.20) | copy-start | bytes 1572868
  7.2 60.7 %all-gather.4.cloned.1.call-start = ((), (), s32[]{:S(2)}) async-start(), calls=%async_computation | async-start | bytes 1916928 | tf_op jit(solution)/shard_map/all_gather | solution.py:79
  8.3 6.9 collective-permute-start
  12.4 5.7 collective-permute-start.1
  20.2 2.3 copy-start.5
  20.2 2.3 copy-start.3
  20.2 4.2 copy-start.4
  22.5 47.8 %copy-start.2 = (bf16[100,1024]{1,0:T(8,128)(2,1)S(1)}, bf16[100,1024]{1,0:T(8,128)(2,1)}, u32[]{:S(2)}) copy-start(bf16[100,1024]{1,0:T(8,128)(2,1)} %param.19) | copy-start | bytes 614404
  23.7 46.7 %copy-start.1 = (bf16[1024,100]{0,1:T(8,128)(2,1)S(1)}, bf16[1024,100]{0,1:T(8,128)(2,1)}, u32[]{:S(2)}) copy-start(bf16[1024,100]{0,1:T(8,128)(2,1)} %get-tuple-element.46) | copy-start | bytes 614404
  23.7 598.7 %all-reduce.3.cloned.1.call-start = ((), (), s32[]{:S(2)}) async-start(), calls=%async_computation.1 | async-start | bytes 2523136
  67.9 2.9 copy-start.7
  70.8 1.2 copy-start.6
  75.2 7.9 %collective-permute-start.2 = (f32[512,64]{0,1:T(8,128)S(1)}, f32[512,64]{0,1:T(8,128)S(1)}, u32[]{:S(2)}, u32[]{:S(2)}) collective-permute-start(f32[512,64]{0,1:T(8,128)S(1)} %get-tuple-element.34), channel_id=1, source_target_pairs={{1,0},{2,1},{3,2},{4,3},{5,4},{6,5},{7,6},{8,7},{9,8},{10,9},{11,1... | collective-permute-start | bytes 393224 | tf_op jit(solution)/shard_map/ppermute | solution.py:30
  79.0 6.3 collective-permute-start.3
Sparse Core Ops, SparseCore 0:
  23.8 44.0 all-gather.3
  74.1 548.2 all-reduce.2
where the time goes:
time: 703 us; the launch traced here: 700 us
  waiting for transfers between devices  584 us (83%)
  blocking collectives  68.5 us (10%)
  between operations  15.6 us (2%)
  starting transfers between devices  10.7 us (2%)
  matrix products  8.6 us (1%)
    unnamed x3, waiting for transfers between devices  536 us
    psum x1, blocking collectives, local(): summed = lax.psum(shard, 'member')  68.5 us
    all_gather x1, waiting for transfers between devices, local(): lax.all_gather(pred[None], 'member', axis=0, tiled=True).astype(jnp.float32)  43.4 us
  transfers between devices with their start and end apart: 6, of which 4 were waited for; matrix products, arithmetic and copies ran while one was open for 1% of the time, Pallas kernels for 0%

commit v1 on v0

v1 whole, which is shorter than its diff:
```python
import functools

import jax
import jax.numpy as jnp
from jax import lax
from jax.experimental import pallas as pl
from jax.experimental.pallas import tpu as pltpu
from jax.sharding import PartitionSpec as P

HALO = 64
LANES = 128
CHUNKS = 2
BLOCKS = 4
ROWS = 48
MAIN = 96
EXTRA = 16
MESH = pl.DeviceIdType.MESH

smooth_sq = 0.01
loss_scale = 4096.0

F32 = jnp.float32
BF16 = jnp.bfloat16


def slope(diff):
    return diff * lax.rsqrt(diff * diff + smooth_sq)


def dot(a, b, da, db):
    return lax.dot_general(a, b, (((da,), (db,)), ((), ())), preferred_element_type=F32)


def low_lanes(shape):
    return lax.broadcasted_iota(jnp.int32, shape, 1) < HALO


def pack(tile):
    half = tile.shape[0] // 2
    top, bottom = tile[:half], tile[half:]
    low = low_lanes(top.shape)
    down = jnp.where(low, top, pltpu.roll(bottom, HALO, 1))
    up = jnp.where(low, pltpu.roll(top, HALO, 1), bottom)
    return down, up


def unpack(below, above):
    low = low_lanes(below.shape)
    top = jnp.where(low, below, pltpu.roll(above, HALO, 1))
    bottom = jnp.where(low, pltpu.roll(below, HALO, 1), above)
    return top, bottom


def kernel(
    dims,
    mesh_in, grid_in, src_in, wgt_in, area_in, count_in, target_in, hw_in, ow_in,
    gh_out, go_out, gm_out,
    mesh_v, grid_v, src_v, wgt_v, area_v, count_v, tgt_v, hw_v, ow_v,
    tgt_f, coef_v, hw_t, ow_f, ow_r, ow_t, ext_v, adj_v, x_v, h_v, f_v,
    halo_s, halo_r, ghalo_s, ghalo_r,
    pred_s, pext_s, pred_r, pext_r, grad_s, gext_s, grad_r, gext_r,
    gw_v, eg_v, s0_s, s0_r, s1_s, s1_r, sum_v, s2_s, s2_r, s3_s, s3_r, gh_v, go_v, gm_v,
    load_sem, store_sem, halo_sem, ghalo_sem, p_sem, pe_send, pe_recv, g_sem, ge_send, ge_recv,
    s0_sem, s1_sem, s2_sem, s3_send, s3_recv,
):
    nx, nl, ny = dims
    nodes = mesh_v.shape[1]
    depth = hw_v.shape[0]
    width = depth + LANES
    points = grid_v.shape[1] // CHUNKS
    member, band = lax.axis_index("member"), lax.axis_index("grid")
    zh, core = member // 2, member % 2
    xi, zl, yi = band // (nl * ny), (band // ny) % nl, band % ny
    bands = nx * nl * ny

    def at(zh_=None, core_=None, x_=None, zl_=None, y_=None):
        zh_ = zh if zh_ is None else zh_
        core_ = core if core_ is None else core_
        x_ = xi if x_ is None else x_
        zl_ = zl if zl_ is None else zl_
        y_ = yi if y_ is None else y_
        return (zh_ * 2 + core_, x_ * (nl * ny) + zl_ * ny + y_)

    above = (member, (band + 1) % bands)
    below = (member, (band + bands - 1) % bands)

    def remote(src, dst, sems, i, device):
        return pltpu.make_async_remote_copy(
            src_ref=src, dst_ref=dst, send_sem=sems.at[0, i], recv_sem=sems.at[1, i],
            device_id=device, device_id_type=MESH,
        )

    barrier = pltpu.get_barrier_semaphore()
    partners = [above, below]
    partners += [at(x_=(xi + s) % nx) for s in range(1, nx)]
    partners += [at(y_=(yi + s) % ny) for s in range(1, ny)]
    partners += [
        at(zh_=(zh + a) % 4, core_=(core + b) % 2, zl_=(zl + c) % nl)
        for a in range(4) for b in range(2) for c in range(nl) if (a, b, c) != (0, 0, 0)
    ]
    for partner in partners:
        pl.semaphore_signal(barrier, inc=1, device_id=partner, device_id_type=MESH)

    def load(i, src, dst):
        copy = pltpu.make_async_copy(src, dst, load_sem.at[i])
        copy.start()
        return copy

    load_mesh = load(0, mesh_in.at[0], mesh_v)
    load_src = load(1, src_in, src_v)
    load_wgt = load(2, wgt_in, wgt_v)
    load_hw = load(3, hw_in, hw_v)
    load_ow = load(4, ow_in, ow_v)
    load_grid = load(5, grid_in.at[0], grid_v)
    load_area = load(6, area_in, area_v)
    load_tgt = load(7, target_in, tgt_v)
    load_count = load(8, count_in, count_v)

    load_mesh.wait()
    down, up = pack(mesh_v[...].astype(F32))
    halo_s[0] = down.astype(BF16)
    halo_s[1] = up.astype(BF16)
    pl.semaphore_wait(barrier, len(partners))
    halo_down = remote(halo_s.at[0], halo_r.at[0], halo_sem, 0, below)
    halo_up = remote(halo_s.at[1], halo_r.at[1], halo_sem, 1, above)
    halo_down.start()
    halo_up.start()

    ext_v[:, 0:nodes] = mesh_v[...]

    load_hw.wait()
    hw_t[...] = hw_v[...].astype(F32).T.astype(BF16)
    load_ow.wait()
    count = ow_v.shape[0]
    ow_f[MAIN:LANES] = jnp.zeros((LANES - MAIN, depth), F32)
    ow_f[0:count] = ow_v[...].astype(F32)
    tail = ow_f[MAIN : MAIN + 8]
    tail = tail + pltpu.roll(tail, 4, 0)
    ow_f[MAIN : MAIN + 8] = tail
    ow_f[MAIN + 8 : MAIN + 16] = tail
    ow_t[...] = ow_f[...].astype(BF16)
    ow_r[...] = ow_f[...].T.astype(BF16)

    load_src.wait()
    load_wgt.wait()
    row = lax.broadcasted_iota(jnp.int32, (nodes + 2 * HALO, points), 0)
    slot = jnp.where(row < nodes, row, jnp.where(row < nodes + HALO, row - (nodes + HALO), row - HALO))
    for chunk in range(CHUNKS):
        cols = pl.ds(chunk * points, points)
        adj = jnp.zeros(row.shape, F32)
        for k in range(3):
            source = src_v[pl.ds(k, 1), cols] - band * nodes
            weight = wgt_v[:, cols].astype(F32)[k : k + 1]
            adj = jnp.where(source == slot, weight, adj)
        adj_v[:, cols] = adj.astype(BF16)

    load_tgt.wait()
    tgt_f[0 : tgt_v.shape[0]] = tgt_v[...].astype(F32)
    load_area.wait()
    load_count.wait()
    place = lax.broadcasted_iota(jnp.int32, (1, CHUNKS * points), 1)
    live = (place < count_v[0]).astype(F32)
    coef_v[...] = loss_scale * area_v[...] * live / tgt_v.shape[0]
    group = lax.broadcasted_iota(jnp.int32, (EXTRA, LANES), 0) // 4

    def spread(blocks):
        out = blocks[0]
        for b in range(1, BLOCKS):
            out = jnp.where(group == b, blocks[b], out)
        return out

    load_grid.wait()
    halo_down.wait_recv()
    halo_up.wait_recv()
    top, bottom = unpack(halo_r[1].astype(F32), halo_r[0].astype(F32))
    ext_v[0 : depth // 2, nodes : nodes + 2 * HALO] = top.astype(BF16)
    ext_v[depth // 2 : depth, nodes : nodes + 2 * HALO] = bottom.astype(BF16)

    keepers = (0, 5)
    others = [(a, b) for a in (2, 1, 3, 0) for b in range(2) if (a, b) != (0, 0)]
    sent = []

    def group_device(j):
        return (j, band)

    def my_rows(ref, core_):
        return ref.at[pl.ds(pl.multiple_of(ROWS * core_, 16), ROWS)]

    def forward(chunk):
        cols = pl.ds(chunk * points, points)
        agg = dot(ext_v[...], adj_v[:, cols], 1, 0)
        x_v[:, cols] = (agg + grid_v[:, cols].astype(F32)).astype(BF16)
        pre = dot(hw_t[...], x_v[:, cols], 1, 0)
        sig = 0.5 * jnp.tanh(0.5 * pre) + 0.5
        h_v[:, cols] = (pre * sig).astype(BF16)
        f_v[:, cols] = sig * (1.0 + pre * (1.0 - sig))
        pred = dot(ow_t[...], h_v[:, cols], 1, 0)
        tails = []
        for b in range(BLOCKS):
            block = pred[:, b * LANES : (b + 1) * LANES]
            pred_s[chunk, b] = block[:MAIN].astype(BF16)
            tails.append(block[MAIN : MAIN + EXTRA])
        pext_s[chunk] = spread(tails).astype(BF16)
        copies = []
        for i, (a, b) in enumerate(others):
            z_, c_ = (zh + a) % 4, (core + b) % 2
            copy = remote(my_rows(pred_s.at[chunk, z_], c_), pred_r.at[chunk, member], p_sem, chunk * 7 + i, at(zh_=z_, core_=c_))
            copy.start()
            copies.append(copy)
        keeper = keepers[chunk]

        @pl.when(member != keeper)
        def _():
            pext_copy(chunk).start()

        pred_r[chunk, member] = my_rows(pred_s.at[chunk, zh], core)[...]
        return copies

    def pext_copy(chunk):
        return pltpu.make_async_remote_copy(
            src_ref=pext_s.at[chunk], dst_ref=pext_r.at[chunk, member],
            send_sem=pe_send.at[chunk], recv_sem=pe_recv.at[chunk, member],
            device_id=group_device(keepers[chunk]), device_id_type=MESH,
        )

    def pext_arrival(chunk, j):
        return pltpu.make_async_remote_copy(
            src_ref=pext_s.at[chunk], dst_ref=pext_r.at[chunk, j],
            send_sem=pe_send.at[chunk], recv_sem=pe_recv.at[chunk, j],
            device_id=group_device(j), device_id_type=MESH,
        )

    def gext_copy(chunk, j):
        return pltpu.make_async_remote_copy(
            src_ref=gext_s.at[chunk, j], dst_ref=gext_r.at[chunk],
            send_sem=ge_send.at[chunk, j], recv_sem=ge_recv.at[chunk],
            device_id=group_device(j), device_id_type=MESH,
        )

    def fair(preds, target, weight):
        out = [slope(p - target) * (1.0 / 8.0) for p in preds]
        pairs = [jnp.zeros(target.shape, F32) for _ in preds]
        for i in range(8):
            for j in range(i + 1, 8):
                s = slope(preds[i] - preds[j])
                pairs[i] = pairs[i] + s
                pairs[j] = pairs[j] - s
        return [weight * (o - q * (1.0 / 56.0)) for o, q in zip(out, pairs)]

    def pair_up(chunk, copies):
        for copy in copies:
            copy.wait_recv()
        sent.extend(copies)
        lanes = pl.ds(pl.multiple_of(chunk * points + zh * LANES, LANES), LANES)

        def tile(t, _):
            rows = pl.ds(pl.multiple_of(t * 16, 16), 16)
            target = tgt_f[pl.ds(pl.multiple_of(ROWS * core + t * 16, 16), 16), lanes]
            grads = fair([pred_r[chunk, j, rows].astype(F32) for j in range(8)], target, coef_v[:, lanes])
            for j in range(8):
                grad_s[chunk, j, rows] = grads[j].astype(BF16)
            return 0

        lax.fori_loop(0, ROWS // 16, tile, 0)
        gcopies = []
        for i, (a, b) in enumerate(others):
            z_, c_ = (zh + a) % 4, (core + b) % 2
            copy = remote(grad_s.at[chunk, z_ * 2 + c_], my_rows(grad_r.at[chunk, zh], core), g_sem, chunk * 7 + i, at(zh_=z_, core_=c_))
            copy.start()
            gcopies.append(copy)
        my_rows(grad_r.at[chunk, zh], core)[...] = grad_s[chunk, member]
        keeper = keepers[chunk]

        @pl.when(member == keeper)
        def _():
            pext_r[chunk, keeper] = pext_s[chunk]
            for j in range(8):
                if j != keeper:
                    pext_arrival(chunk, j).wait_recv()
            targets, weights = [], []
            row8 = lax.broadcasted_iota(jnp.int32, (8, LANES), 0)
            for b in range(BLOCKS):
                at_b = pl.ds(chunk * points + b * LANES, LANES)
                tail = tgt_f[MAIN : MAIN + 8, at_b]
                tail = jnp.where(row8 < 4, tail, pltpu.roll(tail, 4, 0))
                targets.append(jnp.concatenate([tail, tail], axis=0))
                weights.append(jnp.broadcast_to(coef_v[:, at_b], (EXTRA, LANES)))
            grads = fair([pext_r[chunk, j].astype(F32) for j in range(8)], spread(targets), spread(weights))
            for j in range(8):
                gext_s[chunk, j] = grads[j].astype(BF16)
            for j in range(8):
                if j != keeper:
                    gext_copy(chunk, j).start()
            gext_r[chunk] = gext_s[chunk, keeper]

        return gcopies

    def backward(chunk, gcopies):
        cols = pl.ds(chunk * points, points)
        for copy in gcopies:
            copy.wait_recv()
        sent.extend(gcopies)
        keeper = keepers[chunk]

        @pl.when(member != keeper)
        def _():
            gext_copy(chunk, 0).wait_recv()

        tail = gext_r[chunk].astype(F32)
        blocks = []
        for b in range(BLOCKS):
            mine = jnp.where(group == b, tail, 0.0).astype(BF16)
            blocks.append(jnp.concatenate([grad_r[chunk, b], mine, jnp.zeros((LANES - MAIN - EXTRA, LANES), BF16)], axis=0))
        gpred = jnp.concatenate(blocks, axis=1)
        dh = dot(ow_r[...], gpred, 1, 0)
        dpre = (dh * f_v[:, cols]).astype(BF16)
        first = dot(x_v[:, cols], dpre, 1, 1)
        second = dot(h_v[:, cols], gpred, 1, 1)
        if chunk == 0:
            gw_v[:, 0:depth] = first
            gw_v[:, depth:width] = second
        else:
            gw_v[:, 0:depth] += first
            gw_v[:, depth:width] += second
        return dpre

    def node_sums(chunk, dpre):
        cols = pl.ds(chunk * points, points)
        dx = dot(hw_v[...], dpre, 1, 0).astype(BF16)
        sums = dot(dx, adj_v[:, cols], 1, 1)
        if chunk == 0:
            eg_v[...] = sums
        else:
            eg_v[...] += sums

    copies = [forward(chunk) for chunk in range(CHUNKS)]
    gcopies = [pair_up(chunk, copies[chunk]) for chunk in range(CHUNKS)]
    for chunk in range(CHUNKS - 1):
        node_sums(chunk, backward(chunk, gcopies[chunk]))
    last = backward(CHUNKS - 1, gcopies[CHUNKS - 1])

    per_x, per_z, per_y = depth // nx, depth // (nx * nl), depth // (nx * nl * ny)

    def part(x_, core_):
        return pl.ds(pl.multiple_of(x_ * per_x + core_ * per_z, 8), per_z)

    for x_ in range(nx):
        s0_s[x_] = gw_v[part(x_, 1 - core), :].astype(BF16)
    s0 = remote(s0_s, s0_r, s0_sem, 0, at(core_=1 - core))
    s0.start()
    sent.append(s0)

    node_sums(CHUNKS - 1, last)
    down, up = pack(eg_v[:, nodes : nodes + 2 * HALO])
    ghalo_s[0] = down.astype(BF16)
    ghalo_s[1] = up.astype(BF16)
    ghalo_down = remote(ghalo_s.at[0], ghalo_r.at[0], ghalo_sem, 0, below)
    ghalo_up = remote(ghalo_s.at[1], ghalo_r.at[1], ghalo_sem, 1, above)

    s0.wait_recv()
    for x_ in range(nx):
        s1_s[x_] = (gw_v[part(x_, core), :] + s0_r[x_].astype(F32)).astype(BF16)
    s1 = []
    for s in range(1, nx):
        x_ = (xi + s) % nx
        copy = remote(s1_s.at[x_], s1_r.at[s - 1], s1_sem, s - 1, at(x_=x_))
        copy.start()
        s1.append(copy)
    ghalo_down.start()
    ghalo_up.start()
    total = gw_v[part(xi, core), :] + s0_r[xi].astype(F32)
    for copy in s1:
        copy.wait_recv()
    sent.extend(s1)
    for s in range(nx - 1):
        total = total + s1_r[s].astype(F32)
    half = 3 * LANES
    for y_ in range(ny):
        rows = total[y_ * per_y : (y_ + 1) * per_y]
        rest = jnp.concatenate([rows[:, half:width], jnp.zeros((per_y, 2 * half - width), F32)], axis=1)
        sum_v[y_] = jnp.concatenate([rows[:, 0:half], rest], axis=0)
        s2_s[y_] = sum_v[y_].astype(BF16)
    s2 = []
    for s in range(1, ny):
        y_ = (yi + s) % ny
        copy = remote(s2_s.at[y_], s2_r.at[s - 1], s2_sem, s - 1, at(y_=y_))
        copy.start()
        s2.append(copy)

    ghalo_down.wait_recv()
    ghalo_up.wait_recv()
    sent.extend([ghalo_down, ghalo_up])
    top, bottom = unpack(ghalo_r[1].astype(F32), ghalo_r[0].astype(F32))
    gm_v[0 : depth // 2] = eg_v[0 : depth // 2, 0:nodes] + top
    gm_v[depth // 2 : depth] = eg_v[depth // 2 : depth, 0:nodes] + bottom
    gm_store = pltpu.make_async_copy(gm_v, gm_out.at[0], store_sem.at[0])
    gm_store.start()

    total = sum_v[yi]
    for copy in s2:
        copy.wait_recv()
    sent.extend(s2)
    for s in range(ny - 1):
        total = total + s2_r[s].astype(F32)
    s3_s[...] = total.astype(BF16)
    here = zh * nl + zl

    def s3_copy(z_, c_, slot):
        return pltpu.make_async_remote_copy(
            src_ref=s3_s, dst_ref=s3_r.at[slot],
            send_sem=s3_send.at[z_ * 2 + c_], recv_sem=s3_recv.at[slot],
            device_id=at(zh_=z_, core_=c_, zl_=core), device_id_type=MESH,
        )

    def is_me(z_, l_, c_):
        return (zh == z_) & (zl == l_) & (core == c_)

    for z_ in range(4):
        for c_ in range(2):

            @pl.when(jnp.logical_not(is_me(z_, core, c_)))
            def _():
                s3_copy(z_, c_, here).start()

            @pl.when(is_me(z_, core, c_))
            def _():
                s3_r[here] = s3_s[...]

    for z_ in range(4):
        for l_ in range(nl):

            @pl.when(jnp.logical_not(is_me(z_, l_, zl)))
            def _():
                s3_copy(0, 0, z_ * nl + l_).wait_recv()

    total = s3_r[0].astype(F32)
    for z_ in range(1, 4 * nl):
        total = total + s3_r[z_].astype(F32)
    gh_v[...] = jnp.concatenate([total[:per_y, 0:half], total[per_y:, 0 : depth - half]], axis=1)
    second = total[per_y:, depth - half : width - half]
    lane = lax.broadcasted_iota(jnp.int32, second.shape, 1)
    tail = jnp.where((lane >= MAIN) & (lane < MAIN + EXTRA), second, 0.0)
    folded = tail
    for b in range(1, BLOCKS):
        folded = folded + pltpu.roll(tail, LANES - 4 * b, 1)
    go_v[...] = jnp.where(lane < MAIN, second, folded)[:, : go_v.shape[1]]
    gh_store = pltpu.make_async_copy(gh_v, gh_out, store_sem.at[1])
    go_store = pltpu.make_async_copy(go_v, go_out, store_sem.at[2])
    gh_store.start()
    go_store.start()

    halo_down.wait_send()
    halo_up.wait_send()
    for copy in sent:
        copy.wait_send()
    for chunk in range(CHUNKS):
        keeper = keepers[chunk]

        @pl.when(member != keeper)
        def _():
            pext_copy(chunk).wait_send()

        @pl.when(member == keeper)
        def _():
            for j in range(8):
                if j != keeper:
                    gext_copy(chunk, j).wait_send()

    for z_ in range(4):
        for c_ in range(2):

            @pl.when(jnp.logical_not(is_me(z_, core, c_)))
            def _():
                s3_copy(z_, c_, here).wait_send()

    gm_store.wait()
    gh_store.wait()
    go_store.wait()


def solution(mesh, dims=(4, 2, 8)):
    def local(mesh_latent, grid_latent, edge_sources, edge_weights, area_weight, band_counts, target, hidden_weight, out_weight):
        nx, nl, ny = dims
        _, depth, nodes = mesh_latent.shape
        points = grid_latent.shape[2]
        per_chunk = points // CHUNKS
        variables = target.shape[0]
        per_x, per_z, per_y = depth // nx, depth // (nx * nl), depth // (nx * nl * ny)
        width = depth + LANES
        area = area_weight.reshape(1, points)
        vm, dma = pltpu.VMEM, pltpu.SemaphoreType.DMA
        scratch = [
            vm((depth, nodes), BF16), vm((depth, points), BF16), vm((3, points), jnp.int32), vm((3, points), BF16),
            vm((1, points), F32), pltpu.SMEM((1,), jnp.int32), vm((variables, points), BF16), vm((depth, depth), BF16), vm((variables, depth), BF16),
            vm((104, points), F32), vm((1, points), F32), vm((depth, depth), BF16), vm((LANES, depth), F32), vm((depth, LANES), BF16), vm((LANES, depth), BF16),
            vm((depth, nodes + 2 * HALO), BF16), vm((nodes + 2 * HALO, points), BF16), vm((depth, points), BF16), vm((depth, points), BF16), vm((depth, points), F32),
            vm((2, depth // 2, LANES), BF16), vm((2, depth // 2, LANES), BF16), vm((2, depth // 2, LANES), BF16), vm((2, depth // 2, LANES), BF16),
            vm((CHUNKS, BLOCKS, MAIN, LANES), BF16), vm((CHUNKS, EXTRA, LANES), BF16), vm((CHUNKS, 8, ROWS, LANES), BF16), vm((CHUNKS, 8, EXTRA, LANES), BF16),
            vm((CHUNKS, 8, ROWS, LANES), BF16), vm((CHUNKS, 8, EXTRA, LANES), BF16), vm((CHUNKS, BLOCKS, MAIN, LANES), BF16), vm((CHUNKS, EXTRA, LANES), BF16),
            vm((depth, width), F32), vm((depth, nodes + 2 * HALO), F32),
            vm((nx, per_z, width), BF16), vm((nx, per_z, width), BF16), vm((nx, per_z, width), BF16), vm((nx - 1, per_z, width), BF16),
            vm((ny, 2 * per_y, 3 * LANES), F32), vm((ny, 2 * per_y, 3 * LANES), BF16), vm((ny - 1, 2 * per_y, 3 * LANES), BF16),
            vm((2 * per_y, 3 * LANES), BF16), vm((4 * nl, 2 * per_y, 3 * LANES), BF16),
            vm((per_y, depth), F32), vm((per_y, variables), F32), vm((depth, nodes), F32),
            dma((9,)), dma((3,)), dma((2, 2)), dma((2, 2)), dma((2, 7 * CHUNKS)), dma((CHUNKS,)), dma((CHUNKS, 8)),
            dma((2, 7 * CHUNKS)), dma((CHUNKS, 8)), dma((CHUNKS,)),
            dma((2, 1)), dma((2, nx - 1)), dma((2, ny - 1)), dma((8,)), dma((4 * nl,)),
        ]
        return pl.pallas_call(
            functools.partial(kernel, dims),
            out_shape=(
                jax.ShapeDtypeStruct((per_y, depth), F32),
                jax.ShapeDtypeStruct((per_y, variables), F32),
                jax.ShapeDtypeStruct((1, depth, nodes), F32),
            ),
            in_specs=[pl.BlockSpec(memory_space=pl.ANY)] * 9,
            out_specs=[pl.BlockSpec(memory_space=pl.ANY)] * 3,
            scratch_shapes=scratch,
            compiler_params=pltpu.CompilerParams(
                collective_id=0, has_side_effects=True, vmem_limit_bytes=62 * 1024 * 1024
            ),
            name="step",
        )(mesh_latent, grid_latent, edge_sources, edge_weights, area, band_counts, target, hidden_weight, out_weight.T)

    return jax.shard_map(
        local,
        mesh=mesh,
        in_specs=(
            P("member", None, "grid"),
            P("member", None, "grid"),
            P(None, "grid"),
            P(None, "grid"),
            P("grid"),
            P("grid"),
            P(None, "grid"),
            P(),
            P(),
        ),
        out_specs=(P("grid", None), P("grid", None), P("member", None, "grid")),
        check_vma=False,
    )
```

time: 703 us -> 60.1 us (0.09)
  waiting for transfers between devices: 584 us -> 0 us
  blocking collectives: 68.5 us -> 0 us
  Pallas kernels: 0 us -> 55 us
  between operations: 15.6 us -> 1.3 us
  starting transfers between devices: 10.7 us -> 0 us
  matrix products: 8.6 us -> 0 us
    unnamed x3 -> x0, waiting for transfers between devices: 536 us -> none
    psum x1 -> x0, blocking collectives: 68.5 us -> none  [local(): summed = lax.psum(shard, 'member')]
    pallas_call x0 -> x1, Pallas kernels: none -> 55 us  [local(): pl.pallas_call(functools.partial(kernel, dims), out_shape=(jax.ShapeDtype...]
    all_gather x1 -> x0, waiting for transfers between devices: 43.4 us -> none  [local(): lax.all_gather(pred[None], 'member', axis=0, tiled=True).astype(jnp.float32)]
    ppermute x4 -> x0, starting transfers between devices: 10.6 us -> none  [the longest x2 5.29 us: from_behind(): lax.ppermute(value, axis, [(source, source + steps) for source in range(f...]
    dot_general x7 -> x0, matrix products: 8.6 us -> none  [the longest x1 2.29 us: local(): lax.dot_general(hidden_weight, x_in, (((0,), (0,)), ((), ())), preferred_...]
  transfers between devices with their start and end apart: 6 -> 0, of which waited for: 4 -> 0; matrix products, arithmetic and copies ran while one was open for 1% -> 0% of each run, Pallas kernels for 0% -> 0%
where the time goes in v1:
time: 60.1 us; the launch traced here: 59.9 us
  Pallas kernels  55 us (92%)
  local copies, waits for them, and re-layouts  3.59 us (6%)
  between operations  1.3 us (2%)
    pallas_call x1, Pallas kernels, local(): pl.pallas_call(functools.partial(kernel, dims), out_shape=(jax.ShapeDtype...  55 us
    unnamed x5, local copies, waits for them, and re-layouts  3.59 us

profile of v1, /device:TPU:1, one launch (start us, length us, event | category | flops | bytes accessed | tf_op | source)
XLA Modules:
  0.0 59.9 jit_solution(141334052535635609)
XLA Ops:
  1.3 55.0 %step.1 = (f32[8,512]{1,0:T(8,128)}, f32[8,100]{1,0:T(8,128)}, f32[1,512,128]{2,1,0:T(8,128)}) custom-call(bf16[1,512,128]{2,1,0:T(8,128)(2,1)} %mesh_in.1, bf16[1,512,1024]{2,1,0:T(8,128)(2,1)} %grid_in.1, s32[3,1024]{1,0:T(4,128)} %src_in.1, bf16[3,1024]{1,0:T(4,128)(2,1)} %wgt_in.1, f32[1,1024]{1,0:T(1,128)} %bitcast.3, s32[1]{0:T(128)S(6)} %copy.15.count_in, ...), custom_call_target="tpu_custom_call" | custom-call | tf_op jit(solution)/shard_map/step/pallas_call | solution.py:509
  56.3 0.0 copy-start
  56.3 1.3 %copy.16 = f32[8,512]{1,0:T(8,128)} copy(f32[8,512]{1,0:T(8,128)} %get-tuple-element.6) | data formatting | bytes 32768
  57.6 0.0 copy-done
  57.6 0.6 copy.17
  58.2 1.7 %copy.18 = f32[1,512,128]{2,1,0:T(8,128)} copy(f32[1,512,128]{2,1,0:T(8,128)} %get-tuple-element.8) | data formatting | bytes 524288
Async XLA Ops:
  56.3 1.3 %copy-start = (f32[8,100]{1,0:T(8,128)S(1)}, f32[8,100]{1,0:T(8,128)}, u32[]{:S(2)}) copy-start(f32[8,100]{1,0:T(8,128)} %get-tuple-element.7) | copy-start | bytes 9604

commit v2 on v1

v2 whole, which is shorter than its diff:
```python
import functools

import jax
import jax.numpy as jnp
from jax import lax
from jax.experimental import pallas as pl
from jax.experimental.pallas import tpu as pltpu
from jax.sharding import PartitionSpec as P

HALO = 64
LANES = 128
CHUNKS = 4
BLOCKS = 2
GROUPS = 4
KEEPERS = (0, 4)
ROWS = 48
MAIN = 96
EXTRA = 16
MESH = pl.DeviceIdType.MESH

smooth_sq = 0.01
loss_scale = 4096.0

F32 = jnp.float32
BF16 = jnp.bfloat16


def slope(diff):
    return diff * lax.rsqrt(diff * diff + smooth_sq)


def dot(a, b, da, db):
    return lax.dot_general(a, b, (((da,), (db,)), ((), ())), preferred_element_type=F32)


def low_lanes(shape):
    return lax.broadcasted_iota(jnp.int32, shape, 1) < HALO


def pack(tile):
    half = tile.shape[0] // 2
    top, bottom = tile[:half], tile[half:]
    low = low_lanes(top.shape)
    down = jnp.where(low, top, pltpu.roll(bottom, HALO, 1))
    up = jnp.where(low, pltpu.roll(top, HALO, 1), bottom)
    return down, up


def unpack(below, above):
    low = low_lanes(below.shape)
    top = jnp.where(low, below, pltpu.roll(above, HALO, 1))
    bottom = jnp.where(low, pltpu.roll(below, HALO, 1), above)
    return top, bottom


def kernel(
    dims,
    mesh_in, grid_in, src_in, wgt_in, area_in, count_in, target_in, hw_in, ow_in,
    gh_out, go_out, gm_out,
    mesh_v, grid_v, src_v, wgt_v, area_v, count_v, tgt_v, hw_v, ow_v,
    tgt_f, coef_v, hw_t, ow_f, ow_r, ow_t, ext_v, adj_v, x_v, h_v, f_v,
    halo_s, halo_r, ghalo_s, ghalo_r,
    pred_s, pext_s, pred_r, pext_r, grad_s, gext_s, grad_r, gext_r,
    gw_v, eg_v, a0_s, a0_r, b0_s, b0_r, a1_f, a1_s, a1_r, b1_f, b1_s, b1_r, a2_f, a2_s, a2_r, b2_f, b2_s, b2_r, s3_s, s3_r,
    load_sem, halo_sem, ghalo_sem, p_send, p_recv, pe_send, pe_recv, g_send, g_recv, ge_send, ge_recv,
    s0_sem, a1_sem, b1_sem, a2_sem, b2_sem, s3_send, s3_recv,
):
    nx, nl, ny = dims
    nodes = mesh_v.shape[1]
    depth = hw_v.shape[0]
    width = depth + LANES
    points = grid_v.shape[1] // CHUNKS
    member, band = lax.axis_index("member"), lax.axis_index("grid")
    zh, core = member // 2, member % 2
    xi, zl, yi = band // (nl * ny), (band // ny) % nl, band % ny
    bands = nx * nl * ny

    def at(zh_=None, core_=None, x_=None, zl_=None, y_=None):
        zh_ = zh if zh_ is None else zh_
        core_ = core if core_ is None else core_
        x_ = xi if x_ is None else x_
        zl_ = zl if zl_ is None else zl_
        y_ = yi if y_ is None else y_
        return (zh_ * 2 + core_, x_ * (nl * ny) + zl_ * ny + y_)

    above = (member, (band + 1) % bands)
    below = (member, (band + bands - 1) % bands)

    def remote(src, dst, sems, i, device):
        return pltpu.make_async_remote_copy(
            src_ref=src, dst_ref=dst, send_sem=sems.at[0, i], recv_sem=sems.at[1, i],
            device_id=device, device_id_type=MESH,
        )

    barrier = pltpu.get_barrier_semaphore()
    partners = [
        at(zh_=(zh + a) % 4, core_=(core + b) % 2, zl_=(zl + c) % nl)
        for a in (2, 1, 3, 0) for b in range(2) for c in range(nl) if (a, b, c) != (0, 0, 0)
    ]
    partners += [at(y_=(yi + s) % ny) for s in range(1, ny)]
    partners += [at(x_=(xi + s) % nx) for s in range(1, nx)]
    partners += [above, below]

    def load(i, src, dst):
        copy = pltpu.make_async_copy(src, dst, load_sem.at[i])
        copy.start()
        return copy

    load_mesh = load(0, mesh_in.at[0], mesh_v)
    for partner in partners:
        pl.semaphore_signal(barrier, inc=1, device_id=partner, device_id_type=MESH)
    load_src = load(1, src_in, src_v)
    load_wgt = load(2, wgt_in, wgt_v)
    load_hw = load(3, hw_in, hw_v)
    load_ow = load(4, ow_in, ow_v)
    load_grid = load(5, grid_in.at[0], grid_v)
    load_area = load(6, area_in, area_v)
    load_tgt = load(7, target_in, tgt_v)
    load_count = load(8, count_in, count_v)

    load_mesh.wait()
    down, up = pack(mesh_v[...].astype(F32))
    halo_s[0] = down.astype(BF16)
    halo_s[1] = up.astype(BF16)
    pl.semaphore_wait(barrier, len(partners))
    halo_down = remote(halo_s.at[0], halo_r.at[0], halo_sem, 0, below)
    halo_up = remote(halo_s.at[1], halo_r.at[1], halo_sem, 1, above)
    halo_down.start()
    halo_up.start()

    ext_v[:, 0:nodes] = mesh_v[...]

    load_hw.wait()
    hw_t[...] = hw_v[...].astype(F32).T.astype(BF16)
    load_ow.wait()
    count = ow_v.shape[0]
    ow_f[MAIN:LANES] = jnp.zeros((LANES - MAIN, depth), F32)
    ow_f[0:count] = ow_v[...].astype(F32)
    tail = ow_f[MAIN : MAIN + 8]
    tail = tail + pltpu.roll(tail, 4, 0)
    ow_f[MAIN : MAIN + 8] = tail
    ow_f[MAIN + 8 : MAIN + 16] = tail
    ow_t[...] = ow_f[...].astype(BF16)
    ow_r[...] = ow_f[...].T.astype(BF16)

    load_src.wait()
    load_wgt.wait()
    row = lax.broadcasted_iota(jnp.int32, (nodes + 2 * HALO, points), 0)
    slot = jnp.where(row < nodes, row, jnp.where(row < nodes + HALO, row - (nodes + HALO), row - HALO))
    for chunk in range(CHUNKS):
        cols = pl.ds(chunk * points, points)
        adj = jnp.zeros(row.shape, F32)
        for k in range(3):
            source = src_v[pl.ds(k, 1), cols] - band * nodes
            weight = wgt_v[:, cols].astype(F32)[k : k + 1]
            adj = jnp.where(source == slot, weight, adj)
        adj_v[:, cols] = adj.astype(BF16)

    load_tgt.wait()
    tgt_f[0 : tgt_v.shape[0]] = tgt_v[...].astype(F32)
    load_area.wait()
    load_count.wait()
    place = lax.broadcasted_iota(jnp.int32, (1, CHUNKS * points), 1)
    live = (place < count_v[0]).astype(F32)
    coef_v[...] = loss_scale * area_v[...] * live / tgt_v.shape[0]
    group = lax.broadcasted_iota(jnp.int32, (EXTRA, LANES), 0) // 4

    def spread(blocks):
        out = blocks[0]
        for b in range(1, GROUPS):
            out = jnp.where(group == b, blocks[b], out)
        return out

    sent = []

    def finish(stage):
        if stage >= 2:
            halo_down.wait_send()
            halo_up.wait_send()
        for copy in sent:
            copy.wait_send()
        if stage >= 3:
            for k in range(CHUNKS):
                for a in range(1, 4):
                    pred_copy(k, (zh + a) % 4).wait_send()
                pl.when(core != k % 2)(functools.partial(left_pred, k))
                pl.when(core == k % 2)(functools.partial(left_grad, k))
            for sc in range(2):
                pl.when(member != KEEPERS[sc])(functools.partial(left_pext, sc))
                pl.when(member == KEEPERS[sc])(functools.partial(left_gext, sc))
        if stage >= 8:
            for z_ in range(4):
                for c_ in range(2):
                    pl.when(jnp.logical_not(is_me(z_, core, c_)))(functools.partial(left_s3, z_, c_))

    def left_pred(k):
        pred_copy(k, zh).wait_send()

    def left_grad(k):
        for i in range(1, 8):
            grad_copy(k, (member + i) % 8).wait_send()

    def left_pext(sc):
        pext_copy(sc).wait_send()

    def left_gext(sc):
        for j in range(8):
            if j != KEEPERS[sc]:
                gext_copy(sc, j).wait_send()

    def left_s3(z_, c_):
        s3_copy(z_, c_, here).wait_send()

    load_grid.wait()
    halo_down.wait_recv()
    halo_up.wait_recv()
    top, bottom = unpack(halo_r[1].astype(F32), halo_r[0].astype(F32))
    ext_v[0 : depth // 2, nodes : nodes + 2 * HALO] = top.astype(BF16)
    ext_v[depth // 2 : depth, nodes : nodes + 2 * HALO] = bottom.astype(BF16)

    def rows_of(z_):
        return pl.ds(pl.multiple_of(ROWS * (z_ // 2), 16), ROWS)

    def pred_copy(k, z_):
        return pltpu.make_async_remote_copy(
            src_ref=pred_s.at[k, z_ % 2, rows_of(z_)], dst_ref=pred_r.at[k // 2, member],
            send_sem=p_send.at[k, z_], recv_sem=p_recv.at[k // 2, member],
            device_id=at(zh_=z_, core_=k % 2), device_id_type=MESH,
        )

    def pred_arrival(k, j):
        return pltpu.make_async_remote_copy(
            src_ref=pred_s.at[k, 0, pl.ds(0, ROWS)], dst_ref=pred_r.at[k // 2, j],
            send_sem=p_send.at[k, 0], recv_sem=p_recv.at[k // 2, j],
            device_id=(j, band), device_id_type=MESH,
        )

    def grad_copy(k, j):
        return pltpu.make_async_remote_copy(
            src_ref=grad_s.at[k // 2, j], dst_ref=grad_r.at[k, zh % 2, rows_of(zh)],
            send_sem=g_send.at[k // 2, j], recv_sem=g_recv.at[k, zh],
            device_id=(j, band), device_id_type=MESH,
        )

    def grad_arrival(k, z_):
        return pltpu.make_async_remote_copy(
            src_ref=grad_s.at[0, 0], dst_ref=grad_r.at[k, z_ % 2, rows_of(z_)],
            send_sem=g_send.at[0, 0], recv_sem=g_recv.at[k, z_],
            device_id=at(zh_=z_, core_=k % 2), device_id_type=MESH,
        )

    def pext_copy(sc):
        return pltpu.make_async_remote_copy(
            src_ref=pext_s.at[sc], dst_ref=pext_r.at[member],
            send_sem=pe_send.at[sc], recv_sem=pe_recv.at[member],
            device_id=(KEEPERS[sc], band), device_id_type=MESH,
        )

    def pext_arrival(sc, j):
        return pltpu.make_async_remote_copy(
            src_ref=pext_s.at[sc], dst_ref=pext_r.at[j],
            send_sem=pe_send.at[sc], recv_sem=pe_recv.at[j],
            device_id=(j, band), device_id_type=MESH,
        )

    def gext_copy(sc, j):
        return pltpu.make_async_remote_copy(
            src_ref=gext_s.at[j], dst_ref=gext_r.at[sc],
            send_sem=ge_send.at[j], recv_sem=ge_recv.at[sc],
            device_id=(j, band), device_id_type=MESH,
        )

    tails = {}

    def forward(k):
        cols = pl.ds(k * points, points)
        agg = dot(ext_v[...], adj_v[:, cols], 1, 0)
        x_v[:, cols] = (agg + grid_v[:, cols].astype(F32)).astype(BF16)
        pre = dot(hw_t[...], x_v[:, cols], 1, 0)
        sig = 0.5 * jnp.tanh(0.5 * pre) + 0.5
        h_v[:, cols] = (pre * sig).astype(BF16)
        f_v[:, cols] = sig * (1.0 + pre * (1.0 - sig))
        pred = dot(ow_t[...], h_v[:, cols], 1, 0)
        for b in range(BLOCKS):
            block = pred[:, b * LANES : (b + 1) * LANES]
            pred_s[k, b] = block[:MAIN].astype(BF16)
            tails[k * BLOCKS + b] = block[MAIN : MAIN + EXTRA]
        for a in (2, 1, 3):
            pred_copy(k, (zh + a) % 4).start()

        @pl.when(core != k % 2)
        def _():
            pred_copy(k, zh).start()

        @pl.when(core == k % 2)
        def _():
            pred_r[k // 2, member] = pred_s[k, zh % 2, rows_of(zh)]

        if k % 2 == 1:
            sc = k // 2
            pext_s[sc] = spread([tails[sc * GROUPS + b] for b in range(GROUPS)]).astype(BF16)

            @pl.when(member != KEEPERS[sc])
            def _():
                pext_copy(sc).start()

    def fair(preds, target, weight):
        out = [slope(p - target) * (1.0 / 8.0) for p in preds]
        pairs = [jnp.zeros(target.shape, F32) for _ in preds]
        for i in range(8):
            for j in range(i + 1, 8):
                s = slope(preds[i] - preds[j])
                pairs[i] = pairs[i] + s
                pairs[j] = pairs[j] - s
        return [weight * (o - q * (1.0 / 56.0)) for o, q in zip(out, pairs)]

    def pair_up(k):
        @pl.when(core == k % 2)
        def _():
            for i in range(1, 8):
                pred_arrival(k, (member + i) % 8).wait_recv()
            lanes = pl.ds(pl.multiple_of(k * points + (zh % 2) * LANES, LANES), LANES)

            def tile(t, _):
                rows = pl.ds(pl.multiple_of(t * 16, 16), 16)
                target = tgt_f[pl.ds(pl.multiple_of(ROWS * (zh // 2) + t * 16, 16), 16), lanes]
                grads = fair([pred_r[k // 2, j, rows].astype(F32) for j in range(8)], target, coef_v[:, lanes])
                for j in range(8):
                    grad_s[k // 2, j, rows] = grads[j].astype(BF16)
                return 0

            lax.fori_loop(0, ROWS // 16, tile, 0)
            for i in (4, 5, 2, 3, 6, 7, 1):
                grad_copy(k, (member + i) % 8).start()
            grad_r[k, zh % 2, rows_of(zh)] = grad_s[k // 2, member]

    def pair_up_tail(sc):
        keeper = KEEPERS[sc]

        @pl.when(member == keeper)
        def _():
            pext_r[keeper] = pext_s[sc]
            for j in range(8):
                if j != keeper:
                    pext_arrival(sc, j).wait_recv()
            targets, weights = [], []
            row8 = lax.broadcasted_iota(jnp.int32, (8, LANES), 0)
            for b in range(GROUPS):
                at_b = pl.ds((sc * GROUPS + b) * LANES, LANES)
                tail = tgt_f[MAIN : MAIN + 8, at_b]
                tail = jnp.where(row8 < 4, tail, pltpu.roll(tail, 4, 0))
                targets.append(jnp.concatenate([tail, tail], axis=0))
                weights.append(jnp.broadcast_to(coef_v[:, at_b], (EXTRA, LANES)))
            grads = fair([pext_r[j].astype(F32) for j in range(8)], spread(targets), spread(weights))
            for j in range(8):
                gext_s[j] = grads[j].astype(BF16)
            for j in range(8):
                if j != keeper:
                    gext_copy(sc, j).start()
            gext_r[sc] = gext_s[keeper]

    def backward(k):
        cols = pl.ds(k * points, points)
        for a in range(1, 4):
            grad_arrival(k, (zh + a) % 4).wait_recv()

        @pl.when(core != k % 2)
        def _():
            grad_arrival(k, zh).wait_recv()

        sc = k // 2
        if k % 2 == 0:

            @pl.when(member != KEEPERS[sc])
            def _():
                gext_copy(sc, 0).wait_recv()

        tail = gext_r[sc].astype(F32)
        blocks = []
        for b in range(BLOCKS):
            mine = jnp.where(group == (k % 2) * BLOCKS + b, tail, 0.0).astype(BF16)
            blocks.append(jnp.concatenate([grad_r[k, b], mine, jnp.zeros((LANES - MAIN - EXTRA, LANES), BF16)], axis=0))
        gpred = jnp.concatenate(blocks, axis=1)
        dh = dot(ow_r[...], gpred, 1, 0)
        dpre = (dh * f_v[:, cols]).astype(BF16)
        return dpre, gpred

    def add(ref, where, value, first):
        if first:
            ref[:, where] = value
        else:
            ref[:, where] += value

    def weight_terms(k, dpre, gpred, left):
        cols = pl.ds(k * points, points)
        if left:
            add(gw_v, pl.ds(0, lead), dot(x_v[:, cols], dpre[:lead], 1, 1), k == 0)
        else:
            add(gw_v, pl.ds(lead, depth - lead), dot(x_v[:, cols], dpre[lead:], 1, 1), k == 0)
            add(gw_v, pl.ds(depth, LANES), dot(h_v[:, cols], gpred, 1, 1), k == 0)

    def node_sums(k, dpre):
        cols = pl.ds(k * points, points)
        dx = dot(hw_v[...], dpre, 1, 0).astype(BF16)
        add(eg_v, slice(None), dot(dx, adj_v[:, cols], 1, 1), k == 0)

    for k in range(CHUNKS):
        forward(k)
    for k in range(CHUNKS):
        pair_up(k)
        if k % 2 == 1:
            pair_up_tail(k // 2)
    lead = 2 * LANES
    per_x, per_z, per_y = depth // nx, depth // (nx * nl), depth // (nx * nl * ny)

    def part(x_, core_):
        return pl.ds(pl.multiple_of(x_ * per_x + core_ * per_z, 8), per_z)

    for k in range(CHUNKS - 1):
        dpre, gpred = backward(k)
        weight_terms(k, dpre, gpred, True)
        weight_terms(k, dpre, gpred, False)
        node_sums(k, dpre)
    last, gpred = backward(CHUNKS - 1)
    weight_terms(CHUNKS - 1, last, gpred, True)
    for x_ in range(nx):
        b0_s[x_] = gw_v[part(x_, 1 - core), 0:lead].astype(BF16)
    b0 = remote(b0_s, b0_r, s0_sem, 0, at(core_=1 - core))
    b0.start()
    weight_terms(CHUNKS - 1, last, gpred, False)
    for x_ in range(nx):
        a0_s[x_] = gw_v[part(x_, 1 - core), lead:width].astype(BF16)
    a0 = remote(a0_s, a0_r, s0_sem, 1, at(core_=1 - core))
    a0.start()
    sent.extend([b0, a0])

    b0.wait_recv()
    for x_ in range(nx):
        total = gw_v[part(x_, core), 0:lead] + b0_r[x_].astype(F32)
        for y_ in range(ny):
            b1_f[y_, x_ * per_y : (x_ + 1) * per_y] = total[y_ * per_y : (y_ + 1) * per_y]
    b1 = []
    for s in (4, 3, 5, 2, 6, 1, 7):
        if s < ny:
            y_ = (yi + s) % ny
            b1_s[y_] = b1_f[y_].astype(BF16)
            copy = remote(b1_s.at[y_], b1_r.at[s - 1], b1_sem, s - 1, at(y_=y_))
            copy.start()
            b1.append(copy)
    a0.wait_recv()
    for x_ in range(nx):
        a1_f[x_] = gw_v[part(x_, core), lead:width] + a0_r[x_].astype(F32)
    a1 = []
    for s in (2, 1, 3):
        if s < nx:
            x_ = (xi + s) % nx
            a1_s[x_] = a1_f[x_].astype(BF16)
            copy = remote(a1_s.at[x_], a1_r.at[s - 1], a1_sem, s - 1, at(x_=x_))
            copy.start()
            a1.append(copy)
    sent.extend(a1 + b1)

    node_sums(CHUNKS - 1, last)
    down, up = pack(eg_v[:, nodes : nodes + 2 * HALO])
    ghalo_s[0] = down.astype(BF16)
    ghalo_s[1] = up.astype(BF16)
    ghalo_down = remote(ghalo_s.at[0], ghalo_r.at[0], ghalo_sem, 0, below)
    ghalo_up = remote(ghalo_s.at[1], ghalo_r.at[1], ghalo_sem, 1, above)
    ghalo_down.start()
    ghalo_up.start()
    sent.extend([ghalo_down, ghalo_up])

    for copy in a1:
        copy.wait_recv()
    total = a1_f[xi]
    for s in range(nx - 1):
        total = total + a1_r[s].astype(F32)
    for y_ in range(ny):
        rows = total[y_ * per_y : (y_ + 1) * per_y]
        rest = jnp.concatenate([rows[:, lead:], jnp.zeros((per_y, LANES), F32)], axis=1)
        a2_f[y_] = jnp.concatenate([rows[:, :lead], rest], axis=0)
        a2_s[y_] = a2_f[y_].astype(BF16)
    a2 = []
    for s in (4, 3, 5, 2, 6, 1, 7):
        if s < ny:
            y_ = (yi + s) % ny
            copy = remote(a2_s.at[y_], a2_r.at[s - 1], a2_sem, s - 1, at(y_=y_))
            copy.start()
            a2.append(copy)
    for copy in b1:
        copy.wait_recv()
    total = b1_f[yi]
    for s in range(ny - 1):
        total = total + b1_r[s].astype(F32)
    for x_ in range(nx):
        rows = total[x_ * per_y : (x_ + 1) * per_y]
        b2_f[x_] = jnp.concatenate([rows[:, :LANES], rows[:, LANES:]], axis=0)
        b2_s[x_] = b2_f[x_].astype(BF16)
    b2 = []
    for s in (2, 1, 3):
        if s < nx:
            x_ = (xi + s) % nx
            copy = remote(b2_s.at[x_], b2_r.at[s - 1], b2_sem, s - 1, at(x_=x_))
            copy.start()
            b2.append(copy)
    sent.extend(a2 + b2)

    ghalo_down.wait_recv()
    ghalo_up.wait_recv()
    top, bottom = unpack(ghalo_r[1].astype(F32), ghalo_r[0].astype(F32))
    gm_out[0, 0 : depth // 2] = eg_v[0 : depth // 2, 0:nodes] + top
    gm_out[0, depth // 2 : depth] = eg_v[depth // 2 : depth, 0:nodes] + bottom

    for copy in b2:
        copy.wait_recv()
    total = b2_f[xi]
    for s in range(nx - 1):
        total = total + b2_r[s].astype(F32)
    s3_s[:, 0:LANES] = total.astype(BF16)
    for copy in a2:
        copy.wait_recv()
    total = a2_f[yi]
    for s in range(ny - 1):
        total = total + a2_r[s].astype(F32)
    s3_s[:, LANES : 3 * LANES] = total.astype(BF16)
    here = zh * nl + zl

    def s3_copy(z_, c_, slot):
        return pltpu.make_async_remote_copy(
            src_ref=s3_s, dst_ref=s3_r.at[slot],
            send_sem=s3_send.at[z_ * 2 + c_], recv_sem=s3_recv.at[slot],
            device_id=at(zh_=z_, core_=c_, zl_=core), device_id_type=MESH,
        )

    def is_me(z_, l_, c_):
        return (zh == z_) & (zl == l_) & (core == c_)

    for z_ in range(4):
        for c_ in range(2):

            @pl.when(jnp.logical_not(is_me(z_, core, c_)))
            def _():
                s3_copy(z_, c_, here).start()

            @pl.when(is_me(z_, core, c_))
            def _():
                s3_r[here] = s3_s[...]

    for z_ in range(4):
        for l_ in range(nl):

            @pl.when(jnp.logical_not(is_me(z_, l_, zl)))
            def _():
                s3_copy(0, 0, z_ * nl + l_).wait_recv()

    total = s3_r[0].astype(F32)
    for z_ in range(1, 4 * nl):
        total = total + s3_r[z_].astype(F32)
    gh_out[:, 0:LANES] = total[:per_y, 0:LANES]
    gh_out[:, LANES:lead] = total[per_y:, 0:LANES]
    gh_out[:, lead:depth] = total[:per_y, LANES : LANES + depth - lead]
    second = total[per_y:, LANES : 2 * LANES]
    lane = lax.broadcasted_iota(jnp.int32, second.shape, 1)
    tail = jnp.where((lane >= MAIN) & (lane < MAIN + EXTRA), second, 0.0)
    folded = tail
    for b in range(1, GROUPS):
        folded = folded + pltpu.roll(tail, LANES - 4 * b, 1)
    go_out[...] = jnp.where(lane < MAIN, second, folded)[:, : go_out.shape[1]]
    finish(99)


def flush(gh_in, go_in, gm_in, gh_out, go_out, gm_out, sem):
    copies = [pltpu.make_async_copy(a, b, sem.at[i]) for i, (a, b) in enumerate(((gm_in, gm_out), (gh_in, gh_out), (go_in, go_out)))]
    for copy in copies:
        copy.start()
    for copy in copies:
        copy.wait()


def solution(mesh, dims=(4, 2, 8)):
    def local(mesh_latent, grid_latent, edge_sources, edge_weights, area_weight, band_counts, target, hidden_weight, out_weight):
        nx, nl, ny = dims
        _, depth, nodes = mesh_latent.shape
        points = grid_latent.shape[2]
        variables = target.shape[0]
        per_x, per_z, per_y = depth // nx, depth // (nx * nl), depth // (nx * nl * ny)
        width, lead = depth + LANES, 2 * LANES
        tall = width - lead
        area = area_weight.reshape(1, points)
        vm, dma = pltpu.VMEM, pltpu.SemaphoreType.DMA
        scratch = [
            vm((depth, nodes), BF16), vm((depth, points), BF16), vm((3, points), jnp.int32), vm((3, points), BF16),
            vm((1, points), F32), pltpu.SMEM((1,), jnp.int32), vm((variables, points), BF16), vm((depth, depth), BF16), vm((variables, depth), BF16),
            vm((104, points), F32), vm((1, points), F32), vm((depth, depth), BF16), vm((LANES, depth), F32), vm((depth, LANES), BF16), vm((LANES, depth), BF16),
            vm((depth, nodes + 2 * HALO), BF16), vm((nodes + 2 * HALO, points), BF16), vm((depth, points), BF16), vm((depth, points), BF16), vm((depth, points), F32),
            vm((2, depth // 2, LANES), BF16), vm((2, depth // 2, LANES), BF16), vm((2, depth // 2, LANES), BF16), vm((2, depth // 2, LANES), BF16),
            vm((CHUNKS, BLOCKS, MAIN, LANES), BF16), vm((2, EXTRA, LANES), BF16), vm((2, 8, ROWS, LANES), BF16), vm((8, EXTRA, LANES), BF16),
            vm((2, 8, ROWS, LANES), BF16), vm((8, EXTRA, LANES), BF16), vm((CHUNKS, BLOCKS, MAIN, LANES), BF16), vm((2, EXTRA, LANES), BF16),
            vm((depth, width), F32), vm((depth, nodes + 2 * HALO), F32),
            vm((nx, per_z, tall), BF16), vm((nx, per_z, tall), BF16), vm((nx, per_z, lead), BF16), vm((nx, per_z, lead), BF16),
            vm((nx, per_z, tall), F32), vm((nx, per_z, tall), BF16), vm((nx - 1, per_z, tall), BF16),
            vm((ny, nx * per_y, lead), F32), vm((ny, nx * per_y, lead), BF16), vm((ny - 1, nx * per_y, lead), BF16),
            vm((ny, 2 * per_y, lead), F32), vm((ny, 2 * per_y, lead), BF16), vm((ny - 1, 2 * per_y, lead), BF16),
            vm((nx, 2 * per_y, LANES), F32), vm((nx, 2 * per_y, LANES), BF16), vm((nx - 1, 2 * per_y, LANES), BF16),
            vm((2 * per_y, 3 * LANES), BF16), vm((4 * nl, 2 * per_y, 3 * LANES), BF16),
            dma((9,)), dma((2, 2)), dma((2, 2)), dma((CHUNKS, 4)), dma((2, 8)), dma((2,)), dma((8,)),
            dma((2, 8)), dma((CHUNKS, 4)), dma((8,)), dma((2,)),
            dma((2, 2)), dma((2, nx - 1)), dma((2, ny - 1)), dma((2, ny - 1)), dma((2, nx - 1)), dma((8,)), dma((4 * nl,)),
        ]
        sums = pl.pallas_call(
            functools.partial(kernel, dims),
            out_shape=(
                pltpu.VMEM((per_y, depth), F32),
                pltpu.VMEM((per_y, variables), F32),
                pltpu.VMEM((1, depth, nodes), F32),
            ),
            in_specs=[pl.BlockSpec(memory_space=pl.ANY)] * 9,
            out_specs=[pl.BlockSpec(memory_space=pltpu.VMEM)] * 3,
            scratch_shapes=scratch,
            compiler_params=pltpu.CompilerParams(
                collective_id=0, has_side_effects=True, vmem_limit_bytes=62 * 1024 * 1024
            ),
            name="step",
        )(mesh_latent, grid_latent, edge_sources, edge_weights, area, band_counts, target, hidden_weight, out_weight.T)
        return pl.pallas_call(
            flush,
            out_shape=tuple(jax.ShapeDtypeStruct(a.shape, F32) for a in sums),
            in_specs=[pl.BlockSpec(memory_space=pl.ANY)] * 3,
            out_specs=[pl.BlockSpec(memory_space=pl.ANY)] * 3,
            scratch_shapes=[dma((3,))],
            compiler_params=pltpu.CompilerParams(vmem_limit_bytes=1024 * 1024),
            name="flush",
        )(*sums)

    return jax.shard_map(
        local,
        mesh=mesh,
        in_specs=(
            P("member", None, "grid"),
            P("member", None, "grid"),
            P(None, "grid"),
            P(None, "grid"),
            P("grid"),
            P("grid"),
            P(None, "grid"),
            P(),
            P(),
        ),
        out_specs=(P("grid", None), P("grid", None), P("member", None, "grid")),
        check_vma=False,
    )
```

time: 60.1 us -> 55.2 us (0.918)
  local copies, waits for them, and re-layouts: 3.59 us -> 0 us
  Pallas kernels: 55 us -> 53.8 us
    unnamed x5 -> x0, local copies, waits for them, and re-layouts: 3.59 us -> none
    pallas_call x1 -> x2, Pallas kernels: 55 us -> 53.8 us  [the longest x1 53.1 us: local(): pl.pallas_call(functools.partial(kernel, dims), out_shape=(pltpu.VMEM((pe...]
where the time goes in v2:
time: 55.2 us; the launch traced here: 55.1 us
  Pallas kernels  53.8 us (97%)
  between operations  1.29 us (2%)
    pallas_call x1, Pallas kernels, local(): pl.pallas_call(functools.partial(kernel, dims), out_shape=(pltpu.VMEM((pe...  53.1 us

profile of v2, /device:TPU:1, one launch (start us, length us, event | category | flops | bytes accessed | tf_op | source)
XLA Modules:
  0.0 55.1 jit_solution(17765625635465372828)
XLA Ops:
  1.3 53.1 %step.1 = (f32[8,512]{1,0:T(8,128)S(1)}, f32[8,100]{1,0:T(8,128)S(1)}, f32[1,512,128]{2,1,0:T(8,128)S(1)}) custom-call(bf16[1,512,128]{2,1,0:T(8,128)(2,1)} %mesh_in.1, bf16[1,512,1024]{2,1,0:T(8,128)(2,1)} %grid_in.1, s32[3,1024]{1,0:T(4,128)} %src_in.1, bf16[3,1024]{1,0:T(4,128)(2,1)} %wgt_in.1, f32[1,1024]{1,0:T(1,128)} %bitcast.3, s32[1]{0:T(128)S(6)} %copy.12.count_in, ...), custom_call_target="tpu_custom_call" | custom-call | tf_op jit(solution)/shard_map/step/pallas_call | solution.py:610
  54.4 0.7 %flush.1 = (f32[8,512]{1,0:T(8,128)}, f32[8,100]{1,0:T(8,128)}, f32[1,512,128]{2,1,0:T(8,128)}) custom-call(f32[8,512]{1,0:T(8,128)S(1)} %get-tuple-element.6.gh_in, f32[8,100]{1,0:T(8,128)S(1)} %get-tuple-element.7.go_in, f32[1,512,128]{2,1,0:T(8,128)S(1)} %get-tuple-element.8.gm_in), custom_call_target="tpu_custom_call" | custom-call | tf_op jit(solution)/shard_map/flush/pallas_call | solution.py:625

commit v3 on v2

--- a/solution.py
+++ b/solution.py
@@ -58,11 +58,11 @@
     mesh_in, grid_in, src_in, wgt_in, area_in, count_in, target_in, hw_in, ow_in,
     gh_out, go_out, gm_out,
     mesh_v, grid_v, src_v, wgt_v, area_v, count_v, tgt_v, hw_v, ow_v,
-    tgt_f, coef_v, hw_t, ow_f, ow_r, ow_t, ext_v, adj_v, x_v, h_v, f_v,
+    tgt_f, coef_v, hw_t, ow_f, ow_r, ow_t, halo_v, hh_v, xo_v, po_v, adj_v, x_v, h_v, f_v,
     halo_s, halo_r, ghalo_s, ghalo_r,
     pred_s, pext_s, pred_r, pext_r, grad_s, gext_s, grad_r, gext_r,
-    gw_v, eg_v, a0_s, a0_r, b0_s, b0_r, a1_f, a1_s, a1_r, b1_f, b1_s, b1_r, a2_f, a2_s, a2_r, b2_f, b2_s, b2_r, s3_s, s3_r,
-    load_sem, halo_sem, ghalo_sem, p_send, p_recv, pe_send, pe_recv, g_send, g_recv, ge_send, ge_recv,
+    gw_v, eg_v, dpre_v, dx_v, gp_v, a0_s, a0_r, b0_s, b0_r, a1_f, a1_s, a1_r, b1_f, b1_s, b1_r, a2_f, a2_s, a2_r, b2_f, b2_s, b2_r, s3_s, s3_r,
+    coef_r, ttail_s, ttail_r, tgt_r, t_sem, load_sem, halo_sem, ghalo_sem, p_send, p_recv, pe_send, pe_recv, g_send, g_recv, ge_send, ge_recv,
     s0_sem, a1_sem, b1_sem, a2_sem, b2_sem, s3_send, s3_recv,
 ):
     nx, nl, ny = dims
@@ -93,13 +93,14 @@
         )
 
     barrier = pltpu.get_barrier_semaphore()
-    partners = [
-        at(zh_=(zh + a) % 4, core_=(core + b) % 2, zl_=(zl + c) % nl)
-        for a in (2, 1, 3, 0) for b in range(2) for c in range(nl) if (a, b, c) != (0, 0, 0)
-    ]
-    partners += [at(y_=(yi + s) % ny) for s in range(1, ny)]
+    other = xi * (nl * ny) + (1 - zl) * ny + yi
+    ring = sorted(range(1, ny), key=lambda s: -min(s, ny - s))
+    column = [(a, b, c) for a in (2, 1, 3, 0) for b in range(2) for c in range(nl) if (a, b, c) != (0, 0, 0)]
+    partners = [at(zh_=(zh + a) % 4, core_=(core + b) % 2, zl_=(zl + c) % nl) for a, b, c in column[:4]]
+    partners += [at(y_=(yi + s) % ny) for s in ring]
+    partners += [above, below]
+    partners += [at(zh_=(zh + a) % 4, core_=(core + b) % 2, zl_=(zl + c) % nl) for a, b, c in column[4:]]
     partners += [at(x_=(xi + s) % nx) for s in range(1, nx)]
-    partners += [above, below]
 
     def load(i, src, dst):
         copy = pltpu.make_async_copy(src, dst, load_sem.at[i])
@@ -128,7 +129,6 @@
     halo_down.start()
     halo_up.start()
 
-    ext_v[:, 0:nodes] = mesh_v[...]
 
     load_hw.wait()
     hw_t[...] = hw_v[...].astype(F32).T.astype(BF16)
@@ -161,7 +161,7 @@
     load_area.wait()
     load_count.wait()
     place = lax.broadcasted_iota(jnp.int32, (1, CHUNKS * points), 1)
-    live = (place < count_v[0]).astype(F32)
+    live = (place < count_v[...]).astype(F32)
     coef_v[...] = loss_scale * area_v[...] * live / tgt_v.shape[0]
     group = lax.broadcasted_iota(jnp.int32, (EXTRA, LANES), 0) // 4
 
@@ -171,138 +171,143 @@
             out = jnp.where(group == b, blocks[b], out)
         return out
 
+    def rows_of(z_):
+        return pl.ds(pl.multiple_of(ROWS * (z_ // 2), 16), ROWS)
+
+    row8 = lax.broadcasted_iota(jnp.int32, (8, LANES), 0)
+    for sc in range(2):
+        targets = []
+        for b in range(GROUPS):
+            tail = tgt_f[MAIN : MAIN + 8, pl.ds((sc * GROUPS + b) * LANES, LANES)]
+            tail = jnp.where(row8 < 4, tail, pltpu.roll(tail, 4, 0))
+            targets.append(jnp.concatenate([tail, tail], axis=0))
+        ttail_s[sc] = spread(targets).astype(BF16)
+    mate = at(zl_=1 - zl)
+    lent = [remote(coef_v, coef_r, t_sem, 0, mate), remote(ttail_s, ttail_r, t_sem, 1, mate)]
+    for i in range(2):
+        lanes = pl.ds(pl.multiple_of((2 * i + core) * points + (zh % 2) * LANES, LANES), LANES)
+        lent.append(remote(tgt_v.at[rows_of(zh), lanes], tgt_r.at[i], t_sem, 2 + i, mate))
+    for copy in lent:
+        copy.start()
+
+    turn = 1 + (ny - 2) * core
     sent = []
 
-    def finish(stage):
-        if stage >= 2:
-            halo_down.wait_send()
-            halo_up.wait_send()
+    def halos_left():
+        halo_down.wait_send()
+        halo_up.wait_send()
+
+    def points_left():
+        for k in range(CHUNKS):
+            for z_ in range(4):
+                pred_copy(k, z_).wait_send()
+            pl.when(core == k % 2)(functools.partial(left_grad, k))
+        for sc in range(2):
+            pext_copy(sc).wait_send()
+            pl.when(member == KEEPERS[sc])(functools.partial(left_gext, sc))
+
+    def sent_left():
         for copy in sent:
             copy.wait_send()
-        if stage >= 3:
-            for k in range(CHUNKS):
-                for a in range(1, 4):
-                    pred_copy(k, (zh + a) % 4).wait_send()
-                pl.when(core != k % 2)(functools.partial(left_pred, k))
-                pl.when(core == k % 2)(functools.partial(left_grad, k))
-            for sc in range(2):
-                pl.when(member != KEEPERS[sc])(functools.partial(left_pext, sc))
-                pl.when(member == KEEPERS[sc])(functools.partial(left_gext, sc))
-        if stage >= 8:
-            for z_ in range(4):
-                for c_ in range(2):
-                    pl.when(jnp.logical_not(is_me(z_, core, c_)))(functools.partial(left_s3, z_, c_))
-
-    def left_pred(k):
-        pred_copy(k, zh).wait_send()
+        sent.clear()
+
+    def last_left():
+        for z_ in range(4):
+            for c_ in range(2):
+                pl.when(jnp.logical_not(is_me(z_, core, c_)))(functools.partial(left_s3, z_, c_))
 
     def left_grad(k):
-        for i in range(1, 8):
-            grad_copy(k, (member + i) % 8).wait_send()
-
-    def left_pext(sc):
-        pext_copy(sc).wait_send()
+        for j in range(8):
+            grad_copy(k, j).wait_send()
 
     def left_gext(sc):
         for j in range(8):
-            if j != KEEPERS[sc]:
-                gext_copy(sc, j).wait_send()
+            gext_copy(sc, j).wait_send()
 
     def left_s3(z_, c_):
         s3_copy(z_, c_, here).wait_send()
 
     load_grid.wait()
+    for half in range(2):
+        cols = pl.ds(half * 2 * points, 2 * points)
+        xo_v[:, cols] = dot(mesh_v[...], adj_v[0:nodes, cols], 1, 0) + grid_v[:, cols].astype(F32)
+        po_v[:, cols] = dot(hw_t[...], xo_v[:, cols].astype(BF16), 1, 0)
     halo_down.wait_recv()
     halo_up.wait_recv()
     top, bottom = unpack(halo_r[1].astype(F32), halo_r[0].astype(F32))
-    ext_v[0 : depth // 2, nodes : nodes + 2 * HALO] = top.astype(BF16)
-    ext_v[depth // 2 : depth, nodes : nodes + 2 * HALO] = bottom.astype(BF16)
-
-    def rows_of(z_):
-        return pl.ds(pl.multiple_of(ROWS * (z_ // 2), 16), ROWS)
+    halo_v[0 : depth // 2] = top.astype(BF16)
+    halo_v[depth // 2 : depth] = bottom.astype(BF16)
+    hh_v[...] = dot(hw_t[...], halo_v[...], 1, 0).astype(BF16)
+
+    def toward(o):
+        return (zh + zl + o + core * (3 - 2 * o)) % 4
 
     def pred_copy(k, z_):
         return pltpu.make_async_remote_copy(
             src_ref=pred_s.at[k, z_ % 2, rows_of(z_)], dst_ref=pred_r.at[k // 2, member],
             send_sem=p_send.at[k, z_], recv_sem=p_recv.at[k // 2, member],
-            device_id=at(zh_=z_, core_=k % 2), device_id_type=MESH,
+            device_id=at(zh_=z_, core_=k % 2, zl_=1 - zl), device_id_type=MESH,
         )
 
     def pred_arrival(k, j):
         return pltpu.make_async_remote_copy(
             src_ref=pred_s.at[k, 0, pl.ds(0, ROWS)], dst_ref=pred_r.at[k // 2, j],
             send_sem=p_send.at[k, 0], recv_sem=p_recv.at[k // 2, j],
-            device_id=(j, band), device_id_type=MESH,
+            device_id=(j, other), device_id_type=MESH,
         )
 
     def grad_copy(k, j):
         return pltpu.make_async_remote_copy(
             src_ref=grad_s.at[k // 2, j], dst_ref=grad_r.at[k, zh % 2, rows_of(zh)],
             send_sem=g_send.at[k // 2, j], recv_sem=g_recv.at[k, zh],
-            device_id=(j, band), device_id_type=MESH,
+            device_id=(j, other), device_id_type=MESH,
         )
 
     def grad_arrival(k, z_):
         return pltpu.make_async_remote_copy(
             src_ref=grad_s.at[0, 0], dst_ref=grad_r.at[k, z_ % 2, rows_of(z_)],
             send_sem=g_send.at[0, 0], recv_sem=g_recv.at[k, z_],
-            device_id=at(zh_=z_, core_=k % 2), device_id_type=MESH,
+            device_id=at(zh_=z_, core_=k % 2, zl_=1 - zl), device_id_type=MESH,
         )
 
     def pext_copy(sc):
         return pltpu.make_async_remote_copy(
             src_ref=pext_s.at[sc], dst_ref=pext_r.at[member],
             send_sem=pe_send.at[sc], recv_sem=pe_recv.at[member],
-            device_id=(KEEPERS[sc], band), device_id_type=MESH,
+            device_id=(KEEPERS[sc], other), device_id_type=MESH,
         )
 
     def pext_arrival(sc, j):
         return pltpu.make_async_remote_copy(
             src_ref=pext_s.at[sc], dst_ref=pext_r.at[j],
             send_sem=pe_send.at[sc], recv_sem=pe_recv.at[j],
-            device_id=(j, band), device_id_type=MESH,
+            device_id=(j, other), device_id_type=MESH,
         )
 
     def gext_copy(sc, j):
         return pltpu.make_async_remote_copy(
             src_ref=gext_s.at[j], dst_ref=gext_r.at[sc],
             send_sem=ge_send.at[j], recv_sem=ge_recv.at[sc],
-            device_id=(j, band), device_id_type=MESH,
-        )
-
-    tails = {}
-
-    def forward(k):
-        cols = pl.ds(k * points, points)
-        agg = dot(ext_v[...], adj_v[:, cols], 1, 0)
-        x_v[:, cols] = (agg + grid_v[:, cols].astype(F32)).astype(BF16)
-        pre = dot(hw_t[...], x_v[:, cols], 1, 0)
+            device_id=(j, other), device_id_type=MESH,
+        )
+
+    def forward(sc):
+        cols = pl.ds(sc * 2 * points, 2 * points)
+        pre = po_v[:, cols] + dot(hh_v[...], adj_v[nodes : nodes + 2 * HALO, cols], 1, 0)
         sig = 0.5 * jnp.tanh(0.5 * pre) + 0.5
         h_v[:, cols] = (pre * sig).astype(BF16)
         f_v[:, cols] = sig * (1.0 + pre * (1.0 - sig))
         pred = dot(ow_t[...], h_v[:, cols], 1, 0)
-        for b in range(BLOCKS):
+        tails = []
+        for b in range(GROUPS):
             block = pred[:, b * LANES : (b + 1) * LANES]
-            pred_s[k, b] = block[:MAIN].astype(BF16)
-            tails[k * BLOCKS + b] = block[MAIN : MAIN + EXTRA]
-        for a in (2, 1, 3):
-            pred_copy(k, (zh + a) % 4).start()
-
-        @pl.when(core != k % 2)
-        def _():
-            pred_copy(k, zh).start()
-
-        @pl.when(core == k % 2)
-        def _():
-            pred_r[k // 2, member] = pred_s[k, zh % 2, rows_of(zh)]
-
-        if k % 2 == 1:
-            sc = k // 2
-            pext_s[sc] = spread([tails[sc * GROUPS + b] for b in range(GROUPS)]).astype(BF16)
-
-            @pl.when(member != KEEPERS[sc])
-            def _():
-                pext_copy(sc).start()
+            pred_s[2 * sc + b // BLOCKS, b % BLOCKS] = block[:MAIN].astype(BF16)
+            tails.append(block[MAIN : MAIN + EXTRA])
+        pext_s[sc] = spread(tails).astype(BF16)
+        for k in (2 * sc, 2 * sc + 1):
+            for o in (1, 2, 0, 3):
+                pred_copy(k, toward(o)).start()
+        pext_copy(sc).start()
 
     def fair(preds, target, weight):
         out = [slope(p - target) * (1.0 / 8.0) for p in preds]
@@ -317,95 +322,66 @@
     def pair_up(k):
         @pl.when(core == k % 2)
         def _():
-            for i in range(1, 8):
-                pred_arrival(k, (member + i) % 8).wait_recv()
-            lanes = pl.ds(pl.multiple_of(k * points + (zh % 2) * LANES, LANES), LANES)
+            for j in range(8):
+                pred_arrival(k, j).wait_recv()
+            weight = coef_r[:, pl.ds(pl.multiple_of(k * points + (zh % 2) * LANES, LANES), LANES)]
 
             def tile(t, _):
                 rows = pl.ds(pl.multiple_of(t * 16, 16), 16)
-                target = tgt_f[pl.ds(pl.multiple_of(ROWS * (zh // 2) + t * 16, 16), 16), lanes]
-                grads = fair([pred_r[k // 2, j, rows].astype(F32) for j in range(8)], target, coef_v[:, lanes])
+                target = tgt_r[k // 2, rows].astype(F32)
+                grads = fair([pred_r[k // 2, j, rows].astype(F32) for j in range(8)], target, weight)
                 for j in range(8):
                     grad_s[k // 2, j, rows] = grads[j].astype(BF16)
                 return 0
 
             lax.fori_loop(0, ROWS // 16, tile, 0)
-            for i in (4, 5, 2, 3, 6, 7, 1):
-                grad_copy(k, (member + i) % 8).start()
-            grad_r[k, zh % 2, rows_of(zh)] = grad_s[k // 2, member]
+            for o in (1, 2, 0, 3):
+                for c_ in range(2):
+                    grad_copy(k, toward(o) * 2 + c_).start()
 
     def pair_up_tail(sc):
         keeper = KEEPERS[sc]
 
         @pl.when(member == keeper)
         def _():
-            pext_r[keeper] = pext_s[sc]
             for j in range(8):
-                if j != keeper:
-                    pext_arrival(sc, j).wait_recv()
-            targets, weights = [], []
-            row8 = lax.broadcasted_iota(jnp.int32, (8, LANES), 0)
+                pext_arrival(sc, j).wait_recv()
+            weights = []
             for b in range(GROUPS):
                 at_b = pl.ds((sc * GROUPS + b) * LANES, LANES)
-                tail = tgt_f[MAIN : MAIN + 8, at_b]
-                tail = jnp.where(row8 < 4, tail, pltpu.roll(tail, 4, 0))
-                targets.append(jnp.concatenate([tail, tail], axis=0))
-                weights.append(jnp.broadcast_to(coef_v[:, at_b], (EXTRA, LANES)))
-            grads = fair([pext_r[j].astype(F32) for j in range(8)], spread(targets), spread(weights))
+                weights.append(jnp.broadcast_to(coef_r[:, at_b], (EXTRA, LANES)))
+            grads = fair([pext_r[j].astype(F32) for j in range(8)], ttail_r[sc].astype(F32), spread(weights))
             for j in range(8):
                 gext_s[j] = grads[j].astype(BF16)
             for j in range(8):
-                if j != keeper:
-                    gext_copy(sc, j).start()
-            gext_r[sc] = gext_s[keeper]
-
-    def backward(k):
-        cols = pl.ds(k * points, points)
-        for a in range(1, 4):
-            grad_arrival(k, (zh + a) % 4).wait_recv()
-
-        @pl.when(core != k % 2)
-        def _():
-            grad_arrival(k, zh).wait_recv()
-
-        sc = k // 2
-        if k % 2 == 0:
-
-            @pl.when(member != KEEPERS[sc])
-            def _():
-                gext_copy(sc, 0).wait_recv()
+                gext_copy(sc, j).start()
+
+    def backward(sc):
+        cols = pl.ds(sc * 2 * points, 2 * points)
+        for k in (2 * sc, 2 * sc + 1):
+            for z_ in range(4):
+                grad_arrival(k, z_).wait_recv()
+        gext_copy(sc, 0).wait_recv()
 
         tail = gext_r[sc].astype(F32)
         blocks = []
-        for b in range(BLOCKS):
-            mine = jnp.where(group == (k % 2) * BLOCKS + b, tail, 0.0).astype(BF16)
-            blocks.append(jnp.concatenate([grad_r[k, b], mine, jnp.zeros((LANES - MAIN - EXTRA, LANES), BF16)], axis=0))
+        for b in range(GROUPS):
+            mine = jnp.where(group == b, tail, 0.0).astype(BF16)
+            main = grad_r[2 * sc + b // BLOCKS, b % BLOCKS]
+            blocks.append(jnp.concatenate([main, mine, jnp.zeros((LANES - MAIN - EXTRA, LANES), BF16)], axis=0))
         gpred = jnp.concatenate(blocks, axis=1)
         dh = dot(ow_r[...], gpred, 1, 0)
-        dpre = (dh * f_v[:, cols]).astype(BF16)
-        return dpre, gpred
-
-    def add(ref, where, value, first):
-        if first:
-            ref[:, where] = value
-        else:
-            ref[:, where] += value
-
-    def weight_terms(k, dpre, gpred, left):
-        cols = pl.ds(k * points, points)
-        if left:
-            add(gw_v, pl.ds(0, lead), dot(x_v[:, cols], dpre[:lead], 1, 1), k == 0)
-        else:
-            add(gw_v, pl.ds(lead, depth - lead), dot(x_v[:, cols], dpre[lead:], 1, 1), k == 0)
-            add(gw_v, pl.ds(depth, LANES), dot(h_v[:, cols], gpred, 1, 1), k == 0)
-
-    def node_sums(k, dpre):
-        cols = pl.ds(k * points, points)
-        dx = dot(hw_v[...], dpre, 1, 0).astype(BF16)
-        add(eg_v, slice(None), dot(dx, adj_v[:, cols], 1, 1), k == 0)
-
-    for k in range(CHUNKS):
-        forward(k)
+        dpre_v[:, cols] = (dh * f_v[:, cols]).astype(BF16)
+        gp_v[:, cols] = gpred
+
+    forward(0)
+    forward(1)
+    for half in range(2):
+        cols = pl.ds(half * 2 * points, 2 * points)
+        x_v[:, cols] = (xo_v[:, cols] + dot(halo_v[...], adj_v[nodes : nodes + 2 * HALO, cols], 1, 0)).astype(BF16)
+    for copy in lent:
+        copy.wait_recv()
+    sent.extend(lent)
     for k in range(CHUNKS):
         pair_up(k)
         if k % 2 == 1:
@@ -416,18 +392,18 @@
     def part(x_, core_):
         return pl.ds(pl.multiple_of(x_ * per_x + core_ * per_z, 8), per_z)
 
-    for k in range(CHUNKS - 1):
-        dpre, gpred = backward(k)
-        weight_terms(k, dpre, gpred, True)
-        weight_terms(k, dpre, gpred, False)
-        node_sums(k, dpre)
-    last, gpred = backward(CHUNKS - 1)
-    weight_terms(CHUNKS - 1, last, gpred, True)
+    backward(0)
+    early, late = pl.ds(0, 2 * points), pl.ds(2 * points, 2 * points)
+    gw_v[:, 0:depth] = dot(x_v[:, early], dpre_v[:, early], 1, 1)
+    gw_v[:, depth:width] = dot(h_v[:, early], gp_v[:, early], 1, 1)
+    backward(1)
+    gw_v[:, 0:lead] += dot(x_v[:, late], dpre_v[0:lead, late], 1, 1)
     for x_ in range(nx):
         b0_s[x_] = gw_v[part(x_, 1 - core), 0:lead].astype(BF16)
     b0 = remote(b0_s, b0_r, s0_sem, 0, at(core_=1 - core))
     b0.start()
-    weight_terms(CHUNKS - 1, last, gpred, False)
+    gw_v[:, lead:depth] += dot(x_v[:, late], dpre_v[lead:depth, late], 1, 1)
+    gw_v[:, depth:width] += dot(h_v[:, late], gp_v[:, late], 1, 1)
     for x_ in range(nx):
         a0_s[x_] = gw_v[part(x_, 1 - core), lead:width].astype(BF16)
     a0 = remote(a0_s, a0_r, s0_sem, 1, at(core_=1 - core))
@@ -442,7 +418,7 @@
     b1 = []
     for s in (4, 3, 5, 2, 6, 1, 7):
         if s < ny:
-            y_ = (yi + s) % ny
+            y_ = (yi + s * turn) % ny
             b1_s[y_] = b1_f[y_].astype(BF16)
             copy = remote(b1_s.at[y_], b1_r.at[s - 1], b1_sem, s - 1, at(y_=y_))
             copy.start()
@@ -453,15 +429,17 @@
     a1 = []
     for s in (2, 1, 3):
         if s < nx:
-            x_ = (xi + s) % nx
+            x_ = (xi + s * (1 + (nx - 2) * core)) % nx
             a1_s[x_] = a1_f[x_].astype(BF16)
             copy = remote(a1_s.at[x_], a1_r.at[s - 1], a1_sem, s - 1, at(x_=x_))
             copy.start()
             a1.append(copy)
     sent.extend(a1 + b1)
 
-    node_sums(CHUNKS - 1, last)
-    down, up = pack(eg_v[:, nodes : nodes + 2 * HALO])
+    for half in range(2):
+        cols = pl.ds(half * 2 * points, 2 * points)
+        dx_v[:, cols] = dot(hw_v[...], dpre_v[:, cols], 1, 0).astype(BF16)
+    down, up = pack(dot(dx_v[...], adj_v[nodes : nodes + 2 * HALO], 1, 1))
     ghalo_s[0] = down.astype(BF16)
     ghalo_s[1] = up.astype(BF16)
     ghalo_down = remote(ghalo_s.at[0], ghalo_r.at[0], ghalo_sem, 0, below)
@@ -469,6 +447,9 @@
     ghalo_down.start()
     ghalo_up.start()
     sent.extend([ghalo_down, ghalo_up])
+    eg_v[...] = dot(dx_v[...], adj_v[0:nodes], 1, 1)
+    halos_left()
+    points_left()
 
     for copy in a1:
         copy.wait_recv()
@@ -483,7 +464,7 @@
     a2 = []
     for s in (4, 3, 5, 2, 6, 1, 7):
         if s < ny:
-            y_ = (yi + s) % ny
+            y_ = (yi + s * turn) % ny
             copy = remote(a2_s.at[y_], a2_r.at[s - 1], a2_sem, s - 1, at(y_=y_))
             copy.start()
             a2.append(copy)
@@ -499,17 +480,18 @@
     b2 = []
     for s in (2, 1, 3):
         if s < nx:
-            x_ = (xi + s) % nx
+            x_ = (xi + s * (1 + (nx - 2) * core)) % nx
             copy = remote(b2_s.at[x_], b2_r.at[s - 1], b2_sem, s - 1, at(x_=x_))
             copy.start()
             b2.append(copy)
+    sent_left()
     sent.extend(a2 + b2)
 
     ghalo_down.wait_recv()
     ghalo_up.wait_recv()
     top, bottom = unpack(ghalo_r[1].astype(F32), ghalo_r[0].astype(F32))
-    gm_out[0, 0 : depth // 2] = eg_v[0 : depth // 2, 0:nodes] + top
-    gm_out[0, depth // 2 : depth] = eg_v[depth // 2 : depth, 0:nodes] + bottom
+    gm_out[0, 0 : depth // 2] = eg_v[0 : depth // 2] + top
+    gm_out[0, depth // 2 : depth] = eg_v[depth // 2 : depth] + bottom
 
     for copy in b2:
         copy.wait_recv()
@@ -546,6 +528,7 @@
             def _():
                 s3_r[here] = s3_s[...]
 
+    sent_left()
     for z_ in range(4):
         for l_ in range(nl):
 
@@ -566,7 +549,7 @@
     for b in range(1, GROUPS):
         folded = folded + pltpu.roll(tail, LANES - 4 * b, 1)
     go_out[...] = jnp.where(lane < MAIN, second, folded)[:, : go_out.shape[1]]
-    finish(99)
+    last_left()
 
 
 def flush(gh_in, go_in, gm_in, gh_out, go_out, gm_out, sem):
@@ -590,19 +573,21 @@
         vm, dma = pltpu.VMEM, pltpu.SemaphoreType.DMA
         scratch = [
             vm((depth, nodes), BF16), vm((depth, points), BF16), vm((3, points), jnp.int32), vm((3, points), BF16),
-            vm((1, points), F32), pltpu.SMEM((1,), jnp.int32), vm((variables, points), BF16), vm((depth, depth), BF16), vm((variables, depth), BF16),
+            vm((1, points), F32), vm((1, 1), jnp.int32), vm((variables, points), BF16), vm((depth, depth), BF16), vm((variables, depth), BF16),
             vm((104, points), F32), vm((1, points), F32), vm((depth, depth), BF16), vm((LANES, depth), F32), vm((depth, LANES), BF16), vm((LANES, depth), BF16),
-            vm((depth, nodes + 2 * HALO), BF16), vm((nodes + 2 * HALO, points), BF16), vm((depth, points), BF16), vm((depth, points), BF16), vm((depth, points), F32),
+            vm((depth, 2 * HALO), BF16), vm((depth, 2 * HALO), BF16), vm((depth, points), F32), vm((depth, points), F32),
+            vm((nodes + 2 * HALO, points), BF16), vm((depth, points), BF16), vm((depth, points), BF16), vm((depth, points), F32),
             vm((2, depth // 2, LANES), BF16), vm((2, depth // 2, LANES), BF16), vm((2, depth // 2, LANES), BF16), vm((2, depth // 2, LANES), BF16),
             vm((CHUNKS, BLOCKS, MAIN, LANES), BF16), vm((2, EXTRA, LANES), BF16), vm((2, 8, ROWS, LANES), BF16), vm((8, EXTRA, LANES), BF16),
             vm((2, 8, ROWS, LANES), BF16), vm((8, EXTRA, LANES), BF16), vm((CHUNKS, BLOCKS, MAIN, LANES), BF16), vm((2, EXTRA, LANES), BF16),
-            vm((depth, width), F32), vm((depth, nodes + 2 * HALO), F32),
+            vm((depth, width), F32), vm((depth, nodes), F32), vm((depth, points), BF16), vm((depth, points), BF16), vm((LANES, points), BF16),
             vm((nx, per_z, tall), BF16), vm((nx, per_z, tall), BF16), vm((nx, per_z, lead), BF16), vm((nx, per_z, lead), BF16),
             vm((nx, per_z, tall), F32), vm((nx, per_z, tall), BF16), vm((nx - 1, per_z, tall), BF16),
             vm((ny, nx * per_y, lead), F32), vm((ny, nx * per_y, lead), BF16), vm((ny - 1, nx * per_y, lead), BF16),
             vm((ny, 2 * per_y, lead), F32), vm((ny, 2 * per_y, lead), BF16), vm((ny - 1, 2 * per_y, lead), BF16),
             vm((nx, 2 * per_y, LANES), F32), vm((nx, 2 * per_y, LANES), BF16), vm((nx - 1, 2 * per_y, LANES), BF16),
             vm((2 * per_y, 3 * LANES), BF16), vm((4 * nl, 2 * per_y, 3 * LANES), BF16),
+            vm((1, points), F32), vm((2, EXTRA, LANES), BF16), vm((2, EXTRA, LANES), BF16), vm((2, ROWS, LANES), BF16), dma((2, 4)),
             dma((9,)), dma((2, 2)), dma((2, 2)), dma((CHUNKS, 4)), dma((2, 8)), dma((2,)), dma((8,)),
             dma((2, 8)), dma((CHUNKS, 4)), dma((8,)), dma((2,)),
             dma((2, 2)), dma((2, nx - 1)), dma((2, ny - 1)), dma((2, ny - 1)), dma((2, nx - 1)), dma((8,)), dma((4 * nl,)),
@@ -621,7 +606,7 @@
                 collective_id=0, has_side_effects=True, vmem_limit_bytes=62 * 1024 * 1024
             ),
             name="step",
-        )(mesh_latent, grid_latent, edge_sources, edge_weights, area, band_counts, target, hidden_weight, out_weight.T)
+        )(mesh_latent, grid_latent, edge_sources, edge_weights, area, band_counts.reshape(1, 1), target, hidden_weight, out_weight.T)
         return pl.pallas_call(
             flush,
             out_shape=tuple(jax.ShapeDtypeStruct(a.shape, F32) for a in sums),

time: 55.2 us -> 53.9 us (0.976)
  Pallas kernels: 53.8 us -> 52.4 us
    pallas_call x1, Pallas kernels: 53.1 us -> 51.7 us  [local(): pl.pallas_call(functools.partial(kernel, dims), out_shape=(pltpu.VMEM((pe...]
where the time goes in v3:
time: 53.9 us; the launch traced here: 53.7 us
  Pallas kernels  52.4 us (97%)
  between operations  1.29 us (2%)
    pallas_call x1, Pallas kernels, local(): pl.pallas_call(functools.partial(kernel, dims), out_shape=(pltpu.VMEM((pe...  51.7 us

profile of v3, /device:TPU:1, one launch (start us, length us, event | category | flops | bytes accessed | tf_op | source)
XLA Modules:
  0.0 53.7 jit_solution(14110494661931883485)
XLA Ops:
  1.3 51.7 %step.1 = (f32[8,512]{1,0:T(8,128)S(1)}, f32[8,100]{1,0:T(8,128)S(1)}, f32[1,512,128]{2,1,0:T(8,128)S(1)}) custom-call(bf16[1,512,128]{2,1,0:T(8,128)(2,1)} %mesh_in.1, bf16[1,512,1024]{2,1,0:T(8,128)(2,1)} %grid_in.1, s32[3,1024]{1,0:T(4,128)} %src_in.1, bf16[3,1024]{1,0:T(4,128)(2,1)} %wgt_in.1, f32[1,1024]{1,0:T(1,128)} %bitcast.5, ...), custom_call_target="tpu_custom_call" | custom-call | tf_op jit(solution)/shard_map/step/pallas_call | solution.py:595
  53.0 0.7 %flush.1 = (f32[8,512]{1,0:T(8,128)}, f32[8,100]{1,0:T(8,128)}, f32[1,512,128]{2,1,0:T(8,128)}) custom-call(f32[8,512]{1,0:T(8,128)S(1)} %get-tuple-element.6.gh_in, f32[8,100]{1,0:T(8,128)S(1)} %get-tuple-element.7.go_in, f32[1,512,128]{2,1,0:T(8,128)S(1)} %get-tuple-element.8.gm_in), custom_call_target="tpu_custom_call" | custom-call | tf_op jit(solution)/shard_map/flush/pallas_call | solution.py:610

commit v4 on v3

--- a/solution.py
+++ b/solution.py
@@ -62,7 +62,7 @@
     halo_s, halo_r, ghalo_s, ghalo_r,
     pred_s, pext_s, pred_r, pext_r, grad_s, gext_s, grad_r, gext_r,
     gw_v, eg_v, dpre_v, dx_v, gp_v, a0_s, a0_r, b0_s, b0_r, a1_f, a1_s, a1_r, b1_f, b1_s, b1_r, a2_f, a2_s, a2_r, b2_f, b2_s, b2_r, s3_s, s3_r,
-    coef_r, ttail_s, ttail_r, tgt_r, t_sem, load_sem, halo_sem, ghalo_sem, p_send, p_recv, pe_send, pe_recv, g_send, g_recv, ge_send, ge_recv,
+    near_sem, coef_r, ttail_s, ttail_r, tgt_r, t_sem, load_sem, halo_sem, ghalo_sem, p_send, p_recv, pe_send, pe_recv, g_send, g_recv, ge_send, ge_recv,
     s0_sem, a1_sem, b1_sem, a2_sem, b2_sem, s3_send, s3_recv,
 ):
     nx, nl, ny = dims
@@ -94,13 +94,18 @@
 
     barrier = pltpu.get_barrier_semaphore()
     other = xi * (nl * ny) + (1 - zl) * ny + yi
-    ring = sorted(range(1, ny), key=lambda s: -min(s, ny - s))
     column = [(a, b, c) for a in (2, 1, 3, 0) for b in range(2) for c in range(nl) if (a, b, c) != (0, 0, 0)]
+    beside = [at(y_=(yi + 1) % ny), at(y_=(yi + ny - 1) % ny), at(x_=(xi + 1) % nx), at(x_=(xi + nx - 1) % nx)]
     partners = [at(zh_=(zh + a) % 4, core_=(core + b) % 2, zl_=(zl + c) % nl) for a, b, c in column[:4]]
-    partners += [at(y_=(yi + s) % ny) for s in ring]
-    partners += [above, below]
+    partners += [above, below] + beside
     partners += [at(zh_=(zh + a) % 4, core_=(core + b) % 2, zl_=(zl + c) % nl) for a, b, c in column[4:]]
-    partners += [at(x_=(xi + s) % nx) for s in range(1, nx)]
+
+    def tell(i):
+        for partner in beside if i == 0 else beside[:2]:
+            pl.semaphore_signal(near_sem.at[i], inc=1, device_id=partner, device_id_type=MESH)
+
+    def hear(i):
+        pl.semaphore_wait(near_sem.at[i], 4 if i == 0 else 2)
 
     def load(i, src, dst):
         copy = pltpu.make_async_copy(src, dst, load_sem.at[i])
@@ -128,6 +133,7 @@
     halo_up = remote(halo_s.at[1], halo_r.at[1], halo_sem, 1, above)
     halo_down.start()
     halo_up.start()
+    tell(0)
 
 
     load_hw.wait()
@@ -212,9 +218,13 @@
         sent.clear()
 
     def last_left():
-        for z_ in range(4):
+        for a in range(4):
             for c_ in range(2):
-                pl.when(jnp.logical_not(is_me(z_, core, c_)))(functools.partial(left_s3, z_, c_))
+                left = s3_copy((zh + a) % 4, c_, here)
+                if a == 0:
+                    pl.when(jnp.logical_not((zl == core) & (core == c_)))(left.wait_send)
+                else:
+                    left.wait_send()
 
     def left_grad(k):
         for j in range(8):
@@ -223,9 +233,6 @@
     def left_gext(sc):
         for j in range(8):
             gext_copy(sc, j).wait_send()
-
-    def left_s3(z_, c_):
-        s3_copy(z_, c_, here).wait_send()
 
     load_grid.wait()
     for half in range(2):
@@ -375,6 +382,8 @@
         gp_v[:, cols] = gpred
 
     forward(0)
+    hear(0)
+    tell(1)
     forward(1)
     for half in range(2):
         cols = pl.ds(half * 2 * points, 2 * points)
@@ -382,6 +391,8 @@
     for copy in lent:
         copy.wait_recv()
     sent.extend(lent)
+    hear(1)
+    tell(2)
     for k in range(CHUNKS):
         pair_up(k)
         if k % 2 == 1:
@@ -392,6 +403,7 @@
     def part(x_, core_):
         return pl.ds(pl.multiple_of(x_ * per_x + core_ * per_z, 8), per_z)
 
+    hear(2)
     backward(0)
     early, late = pl.ds(0, 2 * points), pl.ds(2 * points, 2 * points)
     gw_v[:, 0:depth] = dot(x_v[:, early], dpre_v[:, early], 1, 1)
@@ -514,27 +526,28 @@
             device_id=at(zh_=z_, core_=c_, zl_=core), device_id_type=MESH,
         )
 
-    def is_me(z_, l_, c_):
-        return (zh == z_) & (zl == l_) & (core == c_)
-
-    for z_ in range(4):
+    for a in (2, 1, 3):
         for c_ in range(2):
-
-            @pl.when(jnp.logical_not(is_me(z_, core, c_)))
-            def _():
-                s3_copy(z_, c_, here).start()
-
-            @pl.when(is_me(z_, core, c_))
-            def _():
-                s3_r[here] = s3_s[...]
+            s3_copy((zh + a) % 4, c_, here).start()
+    for c_ in range(2):
+        mine = (zl == core) & (core == c_)
+
+        @pl.when(jnp.logical_not(mine))
+        def _():
+            s3_copy(zh, c_, here).start()
+
+        @pl.when(mine)
+        def _():
+            s3_r[here] = s3_s[...]
 
     sent_left()
-    for z_ in range(4):
+    for a in range(4):
         for l_ in range(nl):
-
-            @pl.when(jnp.logical_not(is_me(z_, l_, zl)))
-            def _():
-                s3_copy(0, 0, z_ * nl + l_).wait_recv()
+            arrival = s3_copy(0, 0, (zh + a) % 4 * nl + l_)
+            if a == 0:
+                pl.when(jnp.logical_not((l_ == zl) & (core == zl)))(arrival.wait_recv)
+            else:
+                arrival.wait_recv()
 
     total = s3_r[0].astype(F32)
     for z_ in range(1, 4 * nl):
@@ -587,6 +600,7 @@
             vm((ny, 2 * per_y, lead), F32), vm((ny, 2 * per_y, lead), BF16), vm((ny - 1, 2 * per_y, lead), BF16),
             vm((nx, 2 * per_y, LANES), F32), vm((nx, 2 * per_y, LANES), BF16), vm((nx - 1, 2 * per_y, LANES), BF16),
             vm((2 * per_y, 3 * LANES), BF16), vm((4 * nl, 2 * per_y, 3 * LANES), BF16),
+            pltpu.SemaphoreType.REGULAR((3,)),
             vm((1, points), F32), vm((2, EXTRA, LANES), BF16), vm((2, EXTRA, LANES), BF16), vm((2, ROWS, LANES), BF16), dma((2, 4)),
             dma((9,)), dma((2, 2)), dma((2, 2)), dma((CHUNKS, 4)), dma((2, 8)), dma((2,)), dma((8,)),
             dma((2, 8)), dma((CHUNKS, 4)), dma((8,)), dma((2,)),

time: 53.9 us -> 53.2 us (0.987)
  Pallas kernels: 52.4 us -> 51.7 us
    pallas_call x1, Pallas kernels: 51.7 us -> 51 us  [local(): pl.pallas_call(functools.partial(kernel, dims), out_shape=(pltpu.VMEM((pe...]
where the time goes in v4:
time: 53.2 us; the launch traced here: 53 us
  Pallas kernels  51.7 us (97%)
  between operations  1.29 us (2%)
    pallas_call x1, Pallas kernels, local(): pl.pallas_call(functools.partial(kernel, dims), out_shape=(pltpu.VMEM((pe...  51 us

profile of v4, /device:TPU:1, one launch (start us, length us, event | category | flops | bytes accessed | tf_op | source)
XLA Modules:
  0.0 53.0 jit_solution(3692766693634104191)
XLA Ops:
  1.3 51.0 %step.1 = (f32[8,512]{1,0:T(8,128)S(1)}, f32[8,100]{1,0:T(8,128)S(1)}, f32[1,512,128]{2,1,0:T(8,128)S(1)}) custom-call(bf16[1,512,128]{2,1,0:T(8,128)(2,1)} %mesh_in.1, bf16[1,512,1024]{2,1,0:T(8,128)(2,1)} %grid_in.1, s32[3,1024]{1,0:T(4,128)} %src_in.1, bf16[3,1024]{1,0:T(4,128)(2,1)} %wgt_in.1, f32[1,1024]{1,0:T(1,128)} %bitcast.5, ...), custom_call_target="tpu_custom_call" | custom-call | tf_op jit(solution)/shard_map/step/pallas_call | solution.py:609
  52.3 0.7 %flush.1 = (f32[8,512]{1,0:T(8,128)}, f32[8,100]{1,0:T(8,128)}, f32[1,512,128]{2,1,0:T(8,128)}) custom-call(f32[8,512]{1,0:T(8,128)S(1)} %get-tuple-element.6.gh_in, f32[8,100]{1,0:T(8,128)S(1)} %get-tuple-element.7.go_in, f32[1,512,128]{2,1,0:T(8,128)S(1)} %get-tuple-element.8.gm_in), custom_call_target="tpu_custom_call" | custom-call | tf_op jit(solution)/shard_map/flush/pallas_call | solution.py:624

commit v5 on v4

--- a/solution.py
+++ b/solution.py
@@ -12,7 +12,7 @@
 CHUNKS = 4
 BLOCKS = 2
 GROUPS = 4
-KEEPERS = (0, 4)
+KEEPERS = (4, 6)
 ROWS = 48
 MAIN = 96
 EXTRA = 16
@@ -60,9 +60,9 @@
     mesh_v, grid_v, src_v, wgt_v, area_v, count_v, tgt_v, hw_v, ow_v,
     tgt_f, coef_v, hw_t, ow_f, ow_r, ow_t, halo_v, hh_v, xo_v, po_v, adj_v, x_v, h_v, f_v,
     halo_s, halo_r, ghalo_s, ghalo_r,
-    pred_s, pext_s, pred_r, pext_r, grad_s, gext_s, grad_r, gext_r,
+    pred_s, pext_s, pred_r, pext_r, grad_s, grad_r,
     gw_v, eg_v, dpre_v, dx_v, gp_v, a0_s, a0_r, b0_s, b0_r, a1_f, a1_s, a1_r, b1_f, b1_s, b1_r, a2_f, a2_s, a2_r, b2_f, b2_s, b2_r, s3_s, s3_r,
-    near_sem, coef_r, ttail_s, ttail_r, tgt_r, t_sem, load_sem, halo_sem, ghalo_sem, p_send, p_recv, pe_send, pe_recv, g_send, g_recv, ge_send, ge_recv,
+    near_sem, coef_r, ttail_s, ttail_r, tgt_r, t_sem, load_sem, halo_sem, ghalo_sem, p_send, p_recv, pe_send, pe_recv, g_send, g_recv,
     s0_sem, a1_sem, b1_sem, a2_sem, b2_sem, s3_send, s3_recv,
 ):
     nx, nl, ny = dims
@@ -210,7 +210,6 @@
             pl.when(core == k % 2)(functools.partial(left_grad, k))
         for sc in range(2):
             pext_copy(sc).wait_send()
-            pl.when(member == KEEPERS[sc])(functools.partial(left_gext, sc))
 
     def sent_left():
         for copy in sent:
@@ -227,12 +226,15 @@
                     left.wait_send()
 
     def left_grad(k):
-        for j in range(8):
-            grad_copy(k, j).wait_send()
-
-    def left_gext(sc):
-        for j in range(8):
-            gext_copy(sc, j).wait_send()
+        def left(rows):
+            for j in range(8):
+                grad_copy(k, j, rows).wait_send()
+
+        if k % 2 == 0:
+            pl.when(member == KEEPERS[k // 2])(functools.partial(left, ROWS + EXTRA))
+            pl.when(member != KEEPERS[k // 2])(functools.partial(left, ROWS))
+        else:
+            left(ROWS)
 
     load_grid.wait()
     for half in range(2):
@@ -263,16 +265,17 @@
             device_id=(j, other), device_id_type=MESH,
         )
 
-    def grad_copy(k, j):
-        return pltpu.make_async_remote_copy(
-            src_ref=grad_s.at[k // 2, j], dst_ref=grad_r.at[k, zh % 2, rows_of(zh)],
+    def grad_copy(k, j, rows):
+        return pltpu.make_async_remote_copy(
+            src_ref=grad_s.at[k // 2, j, pl.ds(0, rows)], dst_ref=grad_r.at[k, zh, pl.ds(0, rows)],
             send_sem=g_send.at[k // 2, j], recv_sem=g_recv.at[k, zh],
             device_id=(j, other), device_id_type=MESH,
         )
 
     def grad_arrival(k, z_):
-        return pltpu.make_async_remote_copy(
-            src_ref=grad_s.at[0, 0], dst_ref=grad_r.at[k, z_ % 2, rows_of(z_)],
+        rows = ROWS + EXTRA if 2 * z_ + k % 2 == KEEPERS[k // 2] else ROWS
+        return pltpu.make_async_remote_copy(
+            src_ref=grad_s.at[0, 0, pl.ds(0, rows)], dst_ref=grad_r.at[k, z_, pl.ds(0, rows)],
             send_sem=g_send.at[0, 0], recv_sem=g_recv.at[k, z_],
             device_id=at(zh_=z_, core_=k % 2, zl_=1 - zl), device_id_type=MESH,
         )
@@ -288,13 +291,6 @@
         return pltpu.make_async_remote_copy(
             src_ref=pext_s.at[sc], dst_ref=pext_r.at[j],
             send_sem=pe_send.at[sc], recv_sem=pe_recv.at[j],
-            device_id=(j, other), device_id_type=MESH,
-        )
-
-    def gext_copy(sc, j):
-        return pltpu.make_async_remote_copy(
-            src_ref=gext_s.at[j], dst_ref=gext_r.at[sc],
-            send_sem=ge_send.at[j], recv_sem=ge_recv.at[sc],
             device_id=(j, other), device_id_type=MESH,
         )
 
@@ -342,40 +338,46 @@
                 return 0
 
             lax.fori_loop(0, ROWS // 16, tile, 0)
-            for o in (1, 2, 0, 3):
-                for c_ in range(2):
-                    grad_copy(k, toward(o) * 2 + c_).start()
+            def send(rows):
+                for o in (1, 2, 0, 3):
+                    for c_ in range(2):
+                        grad_copy(k, toward(o) * 2 + c_, rows).start()
+
+            if k % 2 == 0:
+                keeper = KEEPERS[k // 2]
+
+                @pl.when(member == keeper)
+                def _():
+                    pair_up_tail(k // 2)
+                    send(ROWS + EXTRA)
+
+                pl.when(member != keeper)(functools.partial(send, ROWS))
+            else:
+                send(ROWS)
 
     def pair_up_tail(sc):
-        keeper = KEEPERS[sc]
-
-        @pl.when(member == keeper)
-        def _():
-            for j in range(8):
-                pext_arrival(sc, j).wait_recv()
-            weights = []
-            for b in range(GROUPS):
-                at_b = pl.ds((sc * GROUPS + b) * LANES, LANES)
-                weights.append(jnp.broadcast_to(coef_r[:, at_b], (EXTRA, LANES)))
-            grads = fair([pext_r[j].astype(F32) for j in range(8)], ttail_r[sc].astype(F32), spread(weights))
-            for j in range(8):
-                gext_s[j] = grads[j].astype(BF16)
-            for j in range(8):
-                gext_copy(sc, j).start()
+        for j in range(8):
+            pext_arrival(sc, j).wait_recv()
+        weights = []
+        for b in range(GROUPS):
+            at_b = pl.ds((sc * GROUPS + b) * LANES, LANES)
+            weights.append(jnp.broadcast_to(coef_r[:, at_b], (EXTRA, LANES)))
+        grads = fair([pext_r[j].astype(F32) for j in range(8)], ttail_r[sc].astype(F32), spread(weights))
+        for j in range(8):
+            grad_s[sc, j, ROWS : ROWS + EXTRA] = grads[j].astype(BF16)
 
     def backward(sc):
         cols = pl.ds(sc * 2 * points, 2 * points)
         for k in (2 * sc, 2 * sc + 1):
             for z_ in range(4):
                 grad_arrival(k, z_).wait_recv()
-        gext_copy(sc, 0).wait_recv()
-
-        tail = gext_r[sc].astype(F32)
+
+        tail = grad_r[2 * sc, KEEPERS[sc] // 2, ROWS : ROWS + EXTRA].astype(F32)
         blocks = []
         for b in range(GROUPS):
             mine = jnp.where(group == b, tail, 0.0).astype(BF16)
-            main = grad_r[2 * sc + b // BLOCKS, b % BLOCKS]
-            blocks.append(jnp.concatenate([main, mine, jnp.zeros((LANES - MAIN - EXTRA, LANES), BF16)], axis=0))
+            main = [grad_r[2 * sc + b // BLOCKS, b % BLOCKS + 2 * i, 0:ROWS] for i in range(2)]
+            blocks.append(jnp.concatenate([*main, mine, jnp.zeros((LANES - MAIN - EXTRA, LANES), BF16)], axis=0))
         gpred = jnp.concatenate(blocks, axis=1)
         dh = dot(ow_r[...], gpred, 1, 0)
         dpre_v[:, cols] = (dh * f_v[:, cols]).astype(BF16)
@@ -395,8 +397,6 @@
     tell(2)
     for k in range(CHUNKS):
         pair_up(k)
-        if k % 2 == 1:
-            pair_up_tail(k // 2)
     lead = 2 * LANES
     per_x, per_z, per_y = depth // nx, depth // (nx * nl), depth // (nx * nl * ny)
 
@@ -526,19 +526,14 @@
             device_id=at(zh_=z_, core_=c_, zl_=core), device_id_type=MESH,
         )
 
-    for a in (2, 1, 3):
+    for z_ in range(4):
         for c_ in range(2):
-            s3_copy((zh + a) % 4, c_, here).start()
-    for c_ in range(2):
-        mine = (zl == core) & (core == c_)
-
-        @pl.when(jnp.logical_not(mine))
-        def _():
-            s3_copy(zh, c_, here).start()
-
-        @pl.when(mine)
-        def _():
-            s3_r[here] = s3_s[...]
+            mine = (zh == z_) & (zl == core) & (core == c_)
+            pl.when(jnp.logical_not(mine))(s3_copy(z_, c_, here).start)
+
+            @pl.when(mine)
+            def _():
+                s3_r[here] = s3_s[...]
 
     sent_left()
     for a in range(4):
@@ -592,7 +587,7 @@
             vm((nodes + 2 * HALO, points), BF16), vm((depth, points), BF16), vm((depth, points), BF16), vm((depth, points), F32),
             vm((2, depth // 2, LANES), BF16), vm((2, depth // 2, LANES), BF16), vm((2, depth // 2, LANES), BF16), vm((2, depth // 2, LANES), BF16),
             vm((CHUNKS, BLOCKS, MAIN, LANES), BF16), vm((2, EXTRA, LANES), BF16), vm((2, 8, ROWS, LANES), BF16), vm((8, EXTRA, LANES), BF16),
-            vm((2, 8, ROWS, LANES), BF16), vm((8, EXTRA, LANES), BF16), vm((CHUNKS, BLOCKS, MAIN, LANES), BF16), vm((2, EXTRA, LANES), BF16),
+            vm((2, 8, ROWS + EXTRA, LANES), BF16), vm((CHUNKS, 4, ROWS + EXTRA, LANES), BF16),
             vm((depth, width), F32), vm((depth, nodes), F32), vm((depth, points), BF16), vm((depth, points), BF16), vm((LANES, points), BF16),
             vm((nx, per_z, tall), BF16), vm((nx, per_z, tall), BF16), vm((nx, per_z, lead), BF16), vm((nx, per_z, lead), BF16),
             vm((nx, per_z, tall), F32), vm((nx, per_z, tall), BF16), vm((nx - 1, per_z, tall), BF16),
@@ -603,7 +598,7 @@
             pltpu.SemaphoreType.REGULAR((3,)),
             vm((1, points), F32), vm((2, EXTRA, LANES), BF16), vm((2, EXTRA, LANES), BF16), vm((2, ROWS, LANES), BF16), dma((2, 4)),
             dma((9,)), dma((2, 2)), dma((2, 2)), dma((CHUNKS, 4)), dma((2, 8)), dma((2,)), dma((8,)),
-            dma((2, 8)), dma((CHUNKS, 4)), dma((8,)), dma((2,)),
+            dma((2, 8)), dma((CHUNKS, 4)),
             dma((2, 2)), dma((2, nx - 1)), dma((2, ny - 1)), dma((2, ny - 1)), dma((2, nx - 1)), dma((8,)), dma((4 * nl,)),
         ]
         sums = pl.pallas_call(

time: 53.2 us -> 52.9 us (level)
  no operation moved by 1% of the time
where the time goes in v5:
time: 52.9 us; the launch traced here: 52.7 us
  Pallas kernels  51.4 us (97%)
  between operations  1.29 us (2%)
    pallas_call x1, Pallas kernels, local(): pl.pallas_call(functools.partial(kernel, dims), out_shape=(pltpu.VMEM((pe...  50.7 us

profile of v5, /device:TPU:1, one launch (start us, length us, event | category | flops | bytes accessed | tf_op | source)
XLA Modules:
  0.0 52.7 jit_solution(7158083446559921421)
XLA Ops:
  1.3 50.7 %step.1 = (f32[8,512]{1,0:T(8,128)S(1)}, f32[8,100]{1,0:T(8,128)S(1)}, f32[1,512,128]{2,1,0:T(8,128)S(1)}) custom-call(bf16[1,512,128]{2,1,0:T(8,128)(2,1)} %mesh_in.1, bf16[1,512,1024]{2,1,0:T(8,128)(2,1)} %grid_in.1, s32[3,1024]{1,0:T(4,128)} %src_in.1, bf16[3,1024]{1,0:T(4,128)(2,1)} %wgt_in.1, f32[1,1024]{1,0:T(1,128)} %bitcast.5, ...), custom_call_target="tpu_custom_call" | custom-call | tf_op jit(solution)/shard_map/step/pallas_call | solution.py:604
  52.0 0.7 %flush.1 = (f32[8,512]{1,0:T(8,128)}, f32[8,100]{1,0:T(8,128)}, f32[1,512,128]{2,1,0:T(8,128)}) custom-call(f32[8,512]{1,0:T(8,128)S(1)} %get-tuple-element.6.gh_in, f32[8,100]{1,0:T(8,128)S(1)} %get-tuple-element.7.go_in, f32[1,512,128]{2,1,0:T(8,128)S(1)} %get-tuple-element.8.gm_in), custom_call_target="tpu_custom_call" | custom-call | tf_op jit(solution)/shard_map/flush/pallas_call | solution.py:619

commit v6 on v5

--- a/solution.py
+++ b/solution.py
@@ -96,9 +96,8 @@
     other = xi * (nl * ny) + (1 - zl) * ny + yi
     column = [(a, b, c) for a in (2, 1, 3, 0) for b in range(2) for c in range(nl) if (a, b, c) != (0, 0, 0)]
     beside = [at(y_=(yi + 1) % ny), at(y_=(yi + ny - 1) % ny), at(x_=(xi + 1) % nx), at(x_=(xi + nx - 1) % nx)]
-    partners = [at(zh_=(zh + a) % 4, core_=(core + b) % 2, zl_=(zl + c) % nl) for a, b, c in column[:4]]
-    partners += [above, below] + beside
-    partners += [at(zh_=(zh + a) % 4, core_=(core + b) % 2, zl_=(zl + c) % nl) for a, b, c in column[4:]]
+    partners = [above, below] + beside
+    partners += [at(zh_=(zh + a) % 4, core_=(core + b) % 2, zl_=(zl + c) % nl) for a, b, c in column]
 
     def tell(i):
         for partner in beside if i == 0 else beside[:2]:

time: 52.9 us -> 52.9 us (level)
  no operation moved by 1% of the time
where the time goes in v6:
time: 52.9 us; the launch traced here: 52.7 us
  Pallas kernels  51.4 us (97%)
  between operations  1.29 us (2%)
    pallas_call x1, Pallas kernels, local(): pl.pallas_call(functools.partial(kernel, dims), out_shape=(pltpu.VMEM((pe...  50.7 us

profile of v6, /device:TPU:1, one launch (start us, length us, event | category | flops | bytes accessed | tf_op | source)
XLA Modules:
  0.0 52.7 jit_solution(8529266521082765037)
XLA Ops:
  1.3 50.7 %step.1 = (f32[8,512]{1,0:T(8,128)S(1)}, f32[8,100]{1,0:T(8,128)S(1)}, f32[1,512,128]{2,1,0:T(8,128)S(1)}) custom-call(bf16[1,512,128]{2,1,0:T(8,128)(2,1)} %mesh_in.1, bf16[1,512,1024]{2,1,0:T(8,128)(2,1)} %grid_in.1, s32[3,1024]{1,0:T(4,128)} %src_in.1, bf16[3,1024]{1,0:T(4,128)(2,1)} %wgt_in.1, f32[1,1024]{1,0:T(1,128)} %bitcast.5, ...), custom_call_target="tpu_custom_call" | custom-call | tf_op jit(solution)/shard_map/step/pallas_call | solution.py:603
  52.0 0.7 %flush.1 = (f32[8,512]{1,0:T(8,128)}, f32[8,100]{1,0:T(8,128)}, f32[1,512,128]{2,1,0:T(8,128)}) custom-call(f32[8,512]{1,0:T(8,128)S(1)} %get-tuple-element.6.gh_in, f32[8,100]{1,0:T(8,128)S(1)} %get-tuple-element.7.go_in, f32[1,512,128]{2,1,0:T(8,128)S(1)} %get-tuple-element.8.gm_in), custom_call_target="tpu_custom_call" | custom-call | tf_op jit(solution)/shard_map/flush/pallas_call | solution.py:618
